TPU v7x, 32 devices: a whole 2x2x4 slice. The times are simulated.
32 devices in a mesh: lat: 4 (over z), lon: 8 (over y, x, core).
Axes of the slice: x: 2, y: 2, z: 4, core: 2. Of those that a mesh axis runs over, the one named last changes fastest.
Arguments:
- ensemble: float32 [128, 1024, 128], P('lat', 'lon'), may hold values from -6 to 6
- observed: float32 [2, 4, 8, 8], P(None, 'lat', 'lon'), may hold values from -8 to 8
- precision: float32 [2, 4, 8, 8], P(None, 'lat', 'lon'), may hold values from 0.05 to 0.5
- interp_weight: float32 [2, 4, 8, 4, 8], P(None, 'lat', 'lon'), may hold values from 0.1 to 1
- stencil: int32 [2, 4, 8, 4, 8], P(None, 'lat', 'lon'), may hold values from 0 to 4419, as said below
- owned: int32 [2, 4, 8, 8], P(None, 'lat', 'lon'), may hold values from 0 to 1, as said below
- pattern: int32 [2, 4, 8, 5, 8], P(None, 'lat', 'lon'), may hold values 0 or 1
Outputs:
- analysis: float32 [128, 1024, 128], P('lat', 'lon')
Inputs may be any that keep to these rules, and one draw needn't show every extreme that they name: `stencil`: each index names one of the four corners of a 2 x 2 square of cells of the rim-extended tile, in the order (0,0), (0,1), (1,0), (1,1). In each batch and tile the owned slots come first and there is at least one; some tile owns all 8 slots in every batch.
All inputs are finite; a program needn't handle non-finite values. No bound on the sum of `pattern` on one device may be relied on, other than what follows from the above.
Results may differ from a plain program's by a relative error of at most 0.0026.
Values may be sent and summed in bfloat16 or wider, within the bound.
No kernel may reach another device: no remote copies, remote signals or barrier semaphores. Data moves between devices by JAX's collectives and lax.ppermute only.
A program may use at most 64 MiB of HBM per device.

v0:
```python
import functools
import jax
import jax.numpy as jnp
from jax import lax
from jax.experimental import pallas as pl
from jax.experimental.pallas import tpu as pltpu
from jax.sharding import PartitionSpec as P

REACH = 2
WIN = 2 * REACH + 1
SUB = 8
LANES = 128
NEAR = (-1, 0, 1)
AT_ROW, AT_COL, AT_OBS = (4, 5, 6)
F32 = jnp.float32
BF16 = jnp.bfloat16


def start_kernel(
    width, observed, precision, weight, stencil, owned, cells, params_ref, left_ref, right_ref,
    observed_v, precision_v, weight_v, stencil_v, owned_v, left_v, right_v, sems
):
    batches, cols = (observed.shape[0], cells.shape[1])
    pairs = (
        (observed, observed_v),
        (precision, precision_v),
        (weight, weight_v),
        (stencil, stencil_v),
        (owned, owned_v),
        (cells.at[:, pl.ds(0, SUB)], left_v),
        (cells.at[:, pl.ds(cols - SUB, SUB)], right_v),
    )
    copies = [pltpu.make_async_copy(source, target, sems.at[n]) for n, (source, target) in enumerate(pairs)]
    for copy in copies:
        copy.start()
    for copy in copies:
        copy.wait()
    params_ref[...] = jnp.zeros_like(params_ref)
    for b in range(batches):
        root = jnp.sqrt(precision_v[b, 0]) * owned_v[b, 0].astype(F32)
        corner = stencil_v[b, 0, 0, pl.ds(0, 1)].astype(F32)
        row = jnp.floor((corner + 0.5) * (1.0 / width))
        params_ref[b, pl.ds(0, 4), pl.ds(0, SUB)] = weight_v[b, 0, 0] * root
        params_ref[b, pl.ds(AT_ROW, 1), pl.ds(0, SUB)] = row
        params_ref[b, pl.ds(AT_COL, 1), pl.ds(0, SUB)] = corner - row * width
        params_ref[b, pl.ds(AT_OBS, 1), pl.ds(0, SUB)] = observed_v[b, 0] * root
    left_ref[...] = left_v[:, 0, :]
    right_ref[...] = right_v[:, SUB - 1, :]


def clear_rim(pad, rows, cols):
    edge = jnp.zeros((2, cols + 2 * SUB, LANES), F32)
    pad[pl.ds(0, 2)] = edge
    pad[pl.ds(rows + 2, 2)] = edge
    side = jnp.zeros((rows, SUB, LANES), F32)
    pad[pl.ds(2, rows), pl.ds(0, SUB)] = side
    pad[pl.ds(2, rows), pl.ds(SUB + cols, SUB)] = side


def share(pad, number, rows, cols, da, dc, o):
    row = number(AT_ROW, o).astype(jnp.int32) - 1 + da * rows
    col = number(AT_COL, o).astype(jnp.int32) - 1 + dc * cols
    row = jnp.clip(row, -2, rows) + 2
    col = jnp.clip(col, -2, cols) + SUB
    terms = [number(k, o) * pad[row + k // 2, pl.ds(col + k % 2, 1), :] for k in range(4)]
    return (terms[0] + terms[1]) + (terms[2] + terms[3])


def own_shift(number):
    sub = lax.broadcasted_iota(jnp.int32, (SUB, LANES), 0)
    shift = jnp.zeros((SUB, LANES), F32)
    for o in range(SUB):
        shift = jnp.where(sub == o, number(AT_OBS, o), shift)
    return shift


def pad_kernel(cells, pad, sem):
    rows, cols = (cells.shape[0], cells.shape[1])
    copy = pltpu.make_async_copy(cells, pad.at[pl.ds(2, rows), pl.ds(SUB, cols)], sem)
    copy.start()
    clear_rim(pad, rows, cols)
    copy.wait()


def column_kernel(mine, above, below, left, right, pad, out_ref, block, sides, params, sems):
    rows, cols = (pad.shape[0] - 4, pad.shape[1] - 2 * SUB)
    copies = []
    for n, tile in enumerate((above, mine, below)):
        copies.append(pltpu.make_async_copy(tile.at[0], params.at[n], sems.at[n]))
    for copy in copies:
        copy.start()
    sides[...] = jnp.zeros_like(sides)
    sides[0, pl.ds(SUB, rows), :] = left[...]
    sides[1, pl.ds(SUB, rows), :] = right[...]
    for copy in copies:
        copy.wait()
    for n, da in enumerate(NEAR):
        number = lambda kind, o: params[n, kind, o]
        for o in range(SUB):
            total = share(pad, number, rows, cols, da, 0, o)
            row = number(AT_ROW, o).astype(jnp.int32) - 1 + da * rows
            row = jnp.clip(row, -2, rows) + SUB
            col = number(AT_COL, o).astype(jnp.int32)
            for side, at in enumerate((0, cols)):
                for k in (side, side + 2):
                    weight = jnp.where(col == at, number(k, o), 0.0)
                    total = total + weight * sides[side, pl.ds(row + k // 2, 1), :]
            block[pl.ds(n * SUB + o, 1), :] = total
        if da == 0:
            own = pl.ds(n * SUB, SUB)
            block[own, :] = block[own, :] - own_shift(number)
    block[pl.ds(len(NEAR) * SUB, SUB), :] = mine[1]
    for slot in range(out_ref.shape[0]):
        out_ref[slot] = block[...]


def window_start(lat_count, my_lat):
    return 0 if lat_count <= WIN else jnp.clip(my_lat - REACH, 0, lat_count - WIN)


def tile_sum(shares, lat, lon, lat_count, lon_count):
    total = jnp.zeros((SUB, LANES), F32)
    for n, da in enumerate(NEAR):
        source = lat - da
        part = pl.ds(n * SUB, SUB)
        if isinstance(source, int):
            if 0 <= source < lat_count:
                total = total + shares[source * lon_count + lon, part, :]
        else:
            inside = (source >= 0) & (source < lat_count)
            source = jnp.clip(source, 0, lat_count - 1)
            total = total + jnp.where(inside, shares[source * lon_count + lon, part, :], 0.0)
    return total


def row_of(block, j):
    return jnp.broadcast_to(block[j:j + 1, :], (SUB, LANES))


def reciprocal(value):
    guess = pl.reciprocal(value, approx=True)
    return guess * (2.0 - value * guess)


def eliminate(blocks):
    count = len(blocks) - 1
    blocks = list(blocks)
    sub = lax.broadcasted_iota(jnp.int32, (SUB, LANES), 0)
    lane = lax.broadcasted_iota(jnp.int32, (SUB, LANES), 1)
    inverse = []
    for k in range(count):
        here = (lane >= k * SUB) & (lane < (k + 1) * SUB)
        column = [
            [jnp.broadcast_to(blocks[i][:, k * SUB + j:k * SUB + j + 1], (SUB, LANES)) for j in range(SUB)]
            for i in range(k, count + 1)
        ]
        diag = column[0]
        full = jnp.where(here, jnp.where(lane - k * SUB == sub, 1.0, 0.0), blocks[k])
        lower = full
        scale = jnp.zeros((SUB, LANES), F32)
        for j in range(0, SUB, 2):
            a, b, c = (row_of(diag[j], j), row_of(diag[j + 1], j), row_of(diag[j + 1], j + 1))
            det = a * c - b * b
            over_det = reciprocal(det)
            first = jnp.where(sub == j, -c, jnp.where(sub == j + 1, b, diag[j] * c - diag[j + 1] * b))
            second = jnp.where(sub == j, b, jnp.where(sub == j + 1, -a, diag[j + 1] * a - diag[j] * b))
            first, second = (first * over_det, second * over_det)
            other = (sub != j) & (sub != j + 1)
            for n in range(j + 2, SUB):
                diag[n] = jnp.where(other, diag[n], 0.0) - first * row_of(diag[n], j) - second * row_of(diag[n], j + 1)
            full = jnp.where(other, full, 0.0) - first * row_of(full, j) - second * row_of(full, j + 1)
            over_a = reciprocal(a)
            top, bottom = (row_of(lower, j), row_of(lower, j + 1))
            below = sub > j + 1
            lower = lower - jnp.where(sub == j + 1, b * over_a, jnp.where(below, first, 0.0)) * top
            lower = lower - jnp.where(below, second, 0.0) * bottom
            scale = jnp.where(sub == j, lax.rsqrt(a), jnp.where(sub == j + 1, lax.rsqrt(det * over_a), scale))
        inverse.append(jnp.where(lane < (k + 1) * SUB, lower * scale, 0.0))
        pivot = [row_of(full, j) for j in range(SUB)]
        for i in range(k + 1, count + 1):
            terms = [column[i - k][j] * pivot[j] for j in range(SUB)]
            while len(terms) > 1:
                terms = [terms[n] + terms[n + 1] for n in range(0, len(terms), 2)]
            blocks[i] = jnp.where(here, 0.0, blocks[i]) - terms[0]
    return inverse, blocks[count][:1]


def batch_map(batch, lat_count, lon_count, near_ref, pattern_ref):
    held = min(WIN, lat_count)
    my_lat = lax.axis_index("lat")
    start = window_start(lat_count, my_lat)
    marks, value = ([], [])
    for e in range(lon_count):
        for j in range(held):
            value.append(tile_sum(near_ref, start + j, e, lat_count, lon_count))
            offset = start + j - my_lat + REACH
            inside = (offset >= 0) & (offset < WIN)
            mark = jnp.where(inside, pattern_ref[batch, 0, 0, jnp.clip(offset, 0, WIN - 1), e], 0)
            marks.append(jnp.full((SUB, LANES), mark.astype(F32)))
    marks = jnp.concatenate(marks, axis=0)
    value = jnp.concatenate(value, axis=0)
    mean = jnp.mean(value, axis=-1, keepdims=True)
    scaled = (value - mean).astype(BF16)
    innov = (-mean).astype(BF16).astype(F32)
    weighted = scaled.astype(F32) * marks
    proj = jnp.sum((weighted * innov).reshape(-1, SUB, LANES), axis=0)
    proj = jnp.sum(proj, axis=0, keepdims=True)
    gram = lax.dot_general(
        weighted.astype(BF16), scaled, (((0,), (0,)), ((), ())), preferred_element_type=F32
    )
    sub = lax.broadcasted_iota(jnp.int32, (SUB, LANES), 0)
    lane = lax.broadcasted_iota(jnp.int32, (SUB, LANES), 1)
    members = LANES
    blocks = []
    for k in range(members // SUB):
        block = gram[k * SUB:(k + 1) * SUB, :]
        blocks.append(block + jnp.where(lane - k * SUB == sub, members - 1.0, 0.0))
    blocks.append(jnp.broadcast_to(proj, (SUB, LANES)))
    inverse, weights = eliminate(blocks)
    flipped = jnp.concatenate(inverse, axis=0) * (members - 1.0) ** 0.5 - weights
    return flipped - jnp.mean(flipped, axis=-1, keepdims=True) + 1.0 / members


def exact_dot(a, b, contract_b):
    return lax.dot_general(
        a, b, (((1,), (contract_b,)), ((), ())), precision=lax.Precision.HIGHEST, preferred_element_type=F32
    )


def first_kernel(
    batch, lat_count, lon_count, near_ref, pattern_ref, pad, left_ref, mid_ref, right_ref, map_ref,
    later, params, sems
):
    rows, cols = (pad.shape[0] - 4, pad.shape[1] - 2 * SUB)
    my_lat, my_lon = (lax.axis_index("lat"), lax.axis_index("lon"))
    copies = []
    for n, dc in enumerate(NEAR):
        lon = lax.rem(my_lon + dc + lon_count, lon_count)
        for m, da in enumerate(NEAR):
            lat = jnp.clip(my_lat + da, 0, lat_count - 1)
            block = near_ref.at[lat * lon_count + lon, pl.ds(len(NEAR) * SUB, SUB)]
            copies.append(pltpu.make_async_copy(block, params.at[n, m], sems.at[n, m]))
            copies[-1].start()
    for copy in copies:
        copy.wait()
    for n, dc in enumerate(NEAR):
        for m, da in enumerate(NEAR):
            number = lambda kind, o: params[n, m, kind, o]
            for o in range(SUB):
                at = (n * len(NEAR) + m) * SUB + o
                later[pl.ds(at, 1), :] = share(pad, number, rows, cols, da, dc, o)
    flipped = batch_map(batch, lat_count, lon_count, near_ref, pattern_ref)
    map_ref[...] = flipped
    moved = exact_dot(later[...], flipped, 1)
    size = len(NEAR) * SUB
    left_ref[...] = moved[:size]
    mid_ref[...] = moved[size:2 * size]
    right_ref[...] = moved[2 * size:]
    own = pl.ds(SUB, SUB)
    mid_ref[own, :] = mid_ref[own, :] - own_shift(lambda kind, o: params[1, 1, kind, o])


def meet_kernel(mid, from_left, from_right, out_ref):
    total = mid[...] + from_left[...] + from_right[...]
    out_ref[...] = jnp.broadcast_to(total, out_ref.shape)


def last_kernel(
    batch, lat_count, lon_count, near_ref, pattern_ref, map_ref, cells_ref, out_ref, cells, result, cell_sem, out_sem
):
    parts = out_sem.shape[0]
    rows = cells.shape[0] // parts
    copy = pltpu.make_async_copy(cells_ref, cells, cell_sem)
    copy.start()
    flipped = exact_dot(batch_map(batch, lat_count, lon_count, near_ref, pattern_ref), map_ref[...], 0)
    high = flipped.astype(BF16)
    low = (flipped - high.astype(F32)).astype(BF16)
    right = jnp.concatenate(
        [jnp.concatenate([high, high], axis=1), jnp.concatenate([low, jnp.zeros_like(low)], axis=1)], axis=0
    )
    copy.wait()
    copies = []
    for n in range(parts):
        part = pl.ds(n * rows, rows)
        value = cells[part, :]
        upper = value.astype(BF16)
        rest = (value - upper.astype(F32)).astype(BF16)
        both = lax.dot_general(
            jnp.concatenate([upper, rest], axis=1), right, (((1,), (1,)), ((), ())), preferred_element_type=F32
        )
        result[part, :] = both[:, :LANES] + both[:, LANES:]
        copies.append(pltpu.make_async_copy(result.at[part], out_ref.at[part], out_sem.at[n]))
        copies[-1].start()
    for out_copy in copies:
        out_copy.wait()


def local(ensemble, observed, precision, interp_weight, stencil, owned, pattern):
    rows, cols, members = ensemble.shape
    batches = observed.shape[0]
    lat_count, lon_count = (lax.axis_size("lat"), lax.axis_size("lon"))
    tiles = lat_count * lon_count
    column = len(NEAR) * SUB
    vmem = pl.BlockSpec(memory_space=pltpu.VMEM)
    smem = pl.BlockSpec(memory_space=pltpu.SMEM)
    anywhere = pl.BlockSpec(memory_space=pl.ANY)
    hbm = pl.BlockSpec(memory_space=pltpu.HBM)
    limit = pltpu.CompilerParams(vmem_limit_bytes=48 * 1024 * 1024)
    whole = pltpu.CompilerParams(vmem_limit_bytes=63 * 1024 * 1024)

    def shape(*dims):
        return jax.ShapeDtypeStruct(dims, F32)

    def exchange(slots):
        return lax.all_to_all(slots, ("lat", "lon"), split_axis=0, concat_axis=0, tiled=True)

    def to_next(array, axis, step, count, wraps):
        route = [(i, (i + step) % count) for i in range(count) if wraps or 0 <= i + step < count]
        return lax.ppermute(array, axis, route)

    small = (observed, precision, interp_weight, stencil, owned)
    mine, left, right = pl.pallas_call(
        functools.partial(start_kernel, cols + 2),
        out_shape=(shape(batches, SUB, LANES), shape(rows, members), shape(rows, members)),
        in_specs=[hbm] * 6,
        out_specs=(vmem,) * 3,
        scratch_shapes=[pltpu.VMEM(array.shape, array.dtype) for array in small]
        + [pltpu.VMEM((rows, SUB, members), F32)] * 2
        + [pltpu.SemaphoreType.DMA((7,))],
        compiler_params=whole,
        name="start",
    )(*small, ensemble)
    from_left = to_next(right, "lon", 1, lon_count, True)
    from_right = to_next(left, "lon", -1, lon_count, True)
    above = to_next(mine, "lat", 1, lat_count, False)
    below = to_next(mine, "lat", -1, lat_count, False)
    pad = pl.pallas_call(
        pad_kernel,
        out_shape=shape(rows + 4, cols + 2 * SUB, members),
        in_specs=[hbm],
        out_specs=vmem,
        scratch_shapes=[pltpu.SemaphoreType.DMA],
        compiler_params=limit,
        name="pad",
    )(ensemble)
    shares = pl.pallas_call(
        column_kernel,
        out_shape=shape(tiles, column + SUB, members),
        in_specs=[vmem] * 6,
        out_specs=vmem,
        scratch_shapes=[
            pltpu.VMEM((column + SUB, members), F32),
            pltpu.VMEM((2, rows + 2 * SUB, members), F32),
            pltpu.SMEM((3, SUB, LANES), F32),
            pltpu.SemaphoreType.DMA((3,)),
        ],
        compiler_params=limit,
        name="column_shares",
    )(mine, above, below, from_left, from_right, pad)
    near = exchange(shares)
    part = shape(column, members)
    left, mid, right, first_map = pl.pallas_call(
        functools.partial(first_kernel, 0, lat_count, lon_count),
        out_shape=(part, part, part, shape(members, members)),
        in_specs=[vmem, smem, vmem],
        out_specs=(vmem,) * 4,
        scratch_shapes=[
            pltpu.VMEM((len(NEAR) * column, members), F32),
            pltpu.SMEM((3, 3, SUB, LANES), F32),
            pltpu.SemaphoreType.DMA((3, 3)),
        ],
        compiler_params=limit,
        name="first_batch",
    )(near, pattern, pad)
    from_left = to_next(right, "lon", 1, lon_count, True)
    from_right = to_next(left, "lon", -1, lon_count, True)
    shares = pl.pallas_call(
        meet_kernel,
        out_shape=shape(tiles, column, members),
        in_specs=[vmem] * 3,
        out_specs=vmem,
        compiler_params=limit,
        name="meet",
    )(mid, from_left, from_right)
    near = exchange(shares)
    parts = 8
    result = pl.pallas_call(
        functools.partial(last_kernel, 1, lat_count, lon_count),
        out_shape=shape(rows * cols, members),
        in_specs=[vmem, smem, vmem, anywhere],
        out_specs=anywhere,
        scratch_shapes=[
            pltpu.VMEM((rows * cols, members), F32),
            pltpu.VMEM((rows * cols, members), F32),
            pltpu.SemaphoreType.DMA,
            pltpu.SemaphoreType.DMA((parts,)),
        ],
        compiler_params=limit,
        name="second_batch",
    )(near, pattern, first_map, ensemble.reshape(rows * cols, members))
    return result.reshape(rows, cols, members)


def solution(mesh):
    placed = (
        P("lat", "lon", None),
        P(None, "lat", "lon", None),
        P(None, "lat", "lon", None),
        P(None, "lat", "lon", None, None),
        P(None, "lat", "lon", None, None),
        P(None, "lat", "lon", None),
        P(None, "lat", "lon", None, None),
    )
    return jax.shard_map(
        local, mesh=mesh, in_specs=placed, out_specs=P("lat", "lon", None), check_vma=False
    )
```

profile of v0, /device:TPU:0, one launch (start us, length us, event | category | flops | bytes accessed | tf_op | source)
XLA Modules:
  0.0 72.3 jit_solution(9222744564043068224)
XLA Ops:
  0.0 1.7 %start.1 = (f32[2,8,128]{2,1,0:T(8,128)}, f32[32,128]{1,0:T(8,128)}, f32[32,128]{1,0:T(8,128)}) custom-call(f32[2,1,1,8]{3,2,1,0:T(1,128)} %observed.1, f32[2,1,1,8]{3,2,1,0:T(1,128)} %precision.1, f32[2,1,1,4,8]{4,3,2,1,0:T(4,128)} %weight.1, s32[2,1,1,4,8]{4,3,2,1,0:T(4,128)} %stencil.1, s32[2,1,1,8]{3,2,1,0:T(1,128)} %owned.1, f32[32,128,128]{2,1,0:T(8,128)} %cells.3), custom_call_target="tpu_custom_call" | custom-call | tf_op jit(solution)/shard_map/start/pallas_call | solution.py:322
  1.7 0.5 collective-permute-start.2
  2.3 2.9 %collective-permute-start.3 = (f32[32,128]{1,0:T(8,128)}, f32[32,128]{1,0:T(8,128)S(1)}, u32[]{:S(2)}, u32[]{:S(2)}) collective-permute-start(f32[32,128]{1,0:T(8,128)} %get-tuple-element.14), channel_id=1, source_target_pairs={{0,7},{1,0},{2,1},{3,2},{4,3},{5,4},{6,5},{7,6},{8,15},{9,8},{10,9... | collective-permute-start | bytes 49160 | tf_op jit(solution)/shard_map/ppermute | solution.py:319
  5.2 4.2 %collective-permute-start = (f32[2,8,128]{2,1,0:T(8,128)}, f32[2,8,128]{2,1,0:T(8,128)S(1)}, u32[]{:S(2)}, u32[]{:S(2)}) collective-permute-start(f32[2,8,128]{2,1,0:T(8,128)} %get-tuple-element.12.mine), channel_id=1, source_target_pairs={{0,8},{8,16},{16,24},{1,9},{9,17},{17,25},{2,10},{10,18},{18,26},{... | collective-permute-start | bytes 24584 | tf_op jit(solution)/shard_map/ppermute | solution.py:319
  9.4 1.3 %collective-permute-start.1 = (f32[2,8,128]{2,1,0:T(8,128)}, f32[2,8,128]{2,1,0:T(8,128)S(1)}, u32[]{:S(2)}, u32[]{:S(2)}) collective-permute-start(f32[2,8,128]{2,1,0:T(8,128)} %get-tuple-element.12.mine), channel_id=1, source_target_pairs={{8,0},{16,8},{24,16},{9,1},{17,9},{25,17},{10,2},{18,10},{26,18},{... | collective-permute-start | bytes 24584 | tf_op jit(solution)/shard_map/ppermute | solution.py:319
  10.7 0.0 copy-start
  10.7 1.6 %copy-done = f32[32,128,128]{2,1,0:T(8,128)S(1)} copy-done((f32[32,128,128]{2,1,0:T(8,128)S(1)}, f32[32,128,128]{2,1,0:T(8,128)}, u32[]{:S(2)}) %copy-start) | copy-done | bytes 2097176
  12.3 0.0 copy-start.3
  12.3 0.2 pad.1
  12.5 0.0 copy-start.4
  12.5 0.0 collective-permute-done.above
  12.5 2.6 %collective-permute-done.1.below = f32[2,8,128]{2,1,0:T(8,128)S(1)} collective-permute-done((f32[2,8,128]{2,1,0:T(8,128)}, f32[2,8,128]{2,1,0:T(8,128)S(1)}, u32[]{:S(2)}, u32[]{:S(2)}) %collective-permute-start.1) | collective-permute-done | bytes 8224 | tf_op jit(solution)/shard_map/ppermute | solution.py:319
  15.1 0.0 collective-permute-done.2.left
  15.1 0.0 collective-permute-done.3.right
  15.1 0.0 copy-done.3
  15.1 1.0 %column_shares.1 = f32[32,32,128]{2,1,0:T(8,128)S(1)} custom-call(f32[2,8,128]{2,1,0:T(8,128)S(1)} %copy-done.3, f32[2,8,128]{2,1,0:T(8,128)S(1)} %collective-permute-done.above, f32[2,8,128]{2,1,0:T(8,128)S(1)} %collective-permute-done.1.below, f32[32,128]{1,0:T(8,128)S(1)} %collective-permute-done.2.left, f32[32,128]{1,0:T(8,128)S(1)} %collective-permute-done.3.right, ...), custom_call_target="tpu_custom_call" | custom-call | tf_op jit(solution)/shard_map/column_shares/pallas_call | solution.py:346
  16.2 0.0 copy-start.2
  16.2 0.8 %copy-done.2 = f32[32,32,128]{2,1,0:T(8,128)} copy-done((f32[32,32,128]{2,1,0:T(8,128)}, f32[32,32,128]{2,1,0:T(8,128)S(1)}, u32[]{:S(2)}) %copy-start.2) | copy-done | bytes 524312
  17.0 3.9 %all-to-all-start = ((f32[32,32,128]{2,1,0:T(8,128)}), f32[32,32,128]{2,1,0:T(8,128)S(1)}, u32[]{:S(2)}, u32[]{:S(2)}) async-start(f32[32,32,128]{2,1,0:T(8,128)} %copy-done.2), calls=%async_computation | async-start | bytes 1048576 | tf_op jit(solution)/shard_map/all_to_all | solution.py:315
  20.9 0.0 copy-done.4
  20.9 15.5 %all-to-all-done.near_ref = f32[32,32,128]{2,1,0:T(8,128)S(1)} async-done(((f32[32,32,128]{2,1,0:T(8,128)}), f32[32,32,128]{2,1,0:T(8,128)S(1)}, u32[]{:S(2)}, u32[]{:S(2)}) %all-to-all-start) | async-done | bytes 524320 | tf_op jit(solution)/shard_map/all_to_all | solution.py:315
  36.5 0.0 copy-start.1
  36.5 7.5 %first_batch.1 = (f32[24,128]{1,0:T(8,128)S(1)}, f32[24,128]{1,0:T(8,128)S(1)}, f32[24,128]{1,0:T(8,128)S(1)}, f32[128,128]{1,0:T(8,128)S(1)}) custom-call(f32[32,32,128]{2,1,0:T(8,128)S(1)} %all-to-all-done.near_ref, s32[2,1,1,5,8]{4,3,2,1,0:T(8,128)S(1)} %copy.8.pattern_ref, f32[36,144,128]{2,1,0:T(8,128)S(1)} %pad.1), custom_call_target="tpu_custom_call" | custom-call | tf_op jit(solution)/shard_map/first_batch/pallas_call | solution.py:362
  43.9 0.1 collective-permute-start.4
  44.0 2.6 %collective-permute-start.5 = (f32[24,128]{1,0:T(8,128)S(1)}, f32[24,128]{1,0:T(8,128)S(1)}, u32[]{:S(2)}, u32[]{:S(2)}) collective-permute-start(f32[24,128]{1,0:T(8,128)S(1)} %get-tuple-element.17), channel_id=1, source_target_pairs={{0,7},{1,0},{2,1},{3,2},{4,3},{5,4},{6,5},{7,6},{8,15},{9,8},{10,9... | collective-permute-start | bytes 36872 | tf_op jit(solution)/shard_map/ppermute | solution.py:319
  46.6 1.4 %collective-permute-done.4.from_left = f32[24,128]{1,0:T(8,128)S(1)} collective-permute-done((f32[24,128]{1,0:T(8,128)S(1)}, f32[24,128]{1,0:T(8,128)S(1)}, u32[]{:S(2)}, u32[]{:S(2)}) %collective-permute-start.4) | collective-permute-done | bytes 12320 | tf_op jit(solution)/shard_map/ppermute | solution.py:319
  48.0 0.0 collective-permute-done.5.from_right
  48.1 16.7 %all_to_all.10.near_ref = f32[32,24,128]{2,1,0:T(8,128)S(1)} all-to-all(f32[32,24,128]{2,1,0:T(8,128)S(1)} %meet.1), channel_id=1, replica_groups=mesh['lat'=4,'lon'=8] {'lat','lon'}, dimensions={0} | all-to-all | bytes 786432 | tf_op jit(solution)/shard_map/all_to_all | solution.py:315
  64.7 0.0 copy-done.1
  64.7 7.6 %second_batch.1 = f32[4096,128]{1,0:T(8,128)} custom-call(f32[32,24,128]{2,1,0:T(8,128)S(1)} %all_to_all.10.near_ref, s32[2,1,1,5,8]{4,3,2,1,0:T(8,128)S(1)} %copy.8.pattern_ref, f32[128,128]{1,0:T(8,128)S(1)} %get-tuple-element.18.map_ref, f32[4096,128]{1,0:T(8,128)S(1)} %bitcast.2), custom_call_target="tpu_custom_call" | custom-call | tf_op jit(solution)/shard_map/second_batch/pallas_call | solution.py:387
  (2 shorter events, 0.0 us)
Async XLA Ops:
  1.7 13.4 %collective-permute-start.2 = (f32[32,128]{1,0:T(8,128)}, f32[32,128]{1,0:T(8,128)S(1)}, u32[]{:S(2)}, u32[]{:S(2)}) collective-permute-start(f32[32,128]{1,0:T(8,128)} %get-tuple-element.13), channel_id=1, source_target_pairs={{0,1},{1,2},{2,3},{3,4},{4,5},{5,6},{6,7},{7,0},{8,9},{9,10},{10,1... | collective-permute-start | bytes 49160 | tf_op jit(solution)/shard_map/ppermute | solution.py:319
  2.3 12.9 %collective-permute-start.3 = (f32[32,128]{1,0:T(8,128)}, f32[32,128]{1,0:T(8,128)S(1)}, u32[]{:S(2)}, u32[]{:S(2)}) collective-permute-start(f32[32,128]{1,0:T(8,128)} %get-tuple-element.14), channel_id=1, source_target_pairs={{0,7},{1,0},{2,1},{3,2},{4,3},{5,4},{6,5},{7,6},{8,15},{9,8},{10,9... | collective-permute-start | bytes 49160 | tf_op jit(solution)/shard_map/ppermute | solution.py:319
  5.2 7.3 %collective-permute-start = (f32[2,8,128]{2,1,0:T(8,128)}, f32[2,8,128]{2,1,0:T(8,128)S(1)}, u32[]{:S(2)}, u32[]{:S(2)}) collective-permute-start(f32[2,8,128]{2,1,0:T(8,128)} %get-tuple-element.12.mine), channel_id=1, source_target_pairs={{0,8},{8,16},{16,24},{1,9},{9,17},{17,25},{2,10},{10,18},{18,26},{... | collective-permute-start | bytes 24584 | tf_op jit(solution)/shard_map/ppermute | solution.py:319
  9.4 5.8 %collective-permute-start.1 = (f32[2,8,128]{2,1,0:T(8,128)}, f32[2,8,128]{2,1,0:T(8,128)S(1)}, u32[]{:S(2)}, u32[]{:S(2)}) collective-permute-start(f32[2,8,128]{2,1,0:T(8,128)} %get-tuple-element.12.mine), channel_id=1, source_target_pairs={{8,0},{16,8},{24,16},{9,1},{17,9},{25,17},{10,2},{18,10},{26,18},{... | collective-permute-start | bytes 24584 | tf_op jit(solution)/shard_map/ppermute | solution.py:319
  10.7 1.6 %copy-start = (f32[32,128,128]{2,1,0:T(8,128)S(1)}, f32[32,128,128]{2,1,0:T(8,128)}, u32[]{:S(2)}) copy-start(f32[32,128,128]{2,1,0:T(8,128)} %cells.3) | copy-start | bytes 6291460
  12.3 2.9 %copy-start.3 = (f32[2,8,128]{2,1,0:T(8,128)S(1)}, f32[2,8,128]{2,1,0:T(8,128)}, u32[]{:S(2)}) copy-start(f32[2,8,128]{2,1,0:T(8,128)} %get-tuple-element.12.mine) | copy-start | bytes 24580
  12.5 8.5 %copy-start.4 = (s32[2,1,1,5,8]{4,2,3,1,0:T(1,128)S(1)}, s32[2,1,1,5,8]{4,2,3,1,0:T(1,128)}, u32[]{:S(2)}) copy-start(s32[2,1,1,5,8]{4,2,3,1,0:T(1,128)} %param.13) | copy-start | bytes 964
  16.2 0.8 %copy-start.2 = (f32[32,32,128]{2,1,0:T(8,128)}, f32[32,32,128]{2,1,0:T(8,128)S(1)}, u32[]{:S(2)}) copy-start(f32[32,32,128]{2,1,0:T(8,128)S(1)} %column_shares.1) | copy-start | bytes 1572868
  17.0 19.5 %all-to-all-start = ((f32[32,32,128]{2,1,0:T(8,128)}), f32[32,32,128]{2,1,0:T(8,128)S(1)}, u32[]{:S(2)}, u32[]{:S(2)}) async-start(f32[32,32,128]{2,1,0:T(8,128)} %copy-done.2), calls=%async_computation | async-start | bytes 1048576 | tf_op jit(solution)/shard_map/all_to_all | solution.py:315
  36.5 28.3 %copy-start.1 = (f32[32,128,128]{2,1,0:T(8,128)S(1)}, f32[32,128,128]{2,1,0:T(8,128)}, u32[]{:S(2)}) copy-start(f32[32,128,128]{2,1,0:T(8,128)} %cells.3) | copy-start | bytes 6291460
  43.9 4.1 %collective-permute-start.4 = (f32[24,128]{1,0:T(8,128)S(1)}, f32[24,128]{1,0:T(8,128)S(1)}, u32[]{:S(2)}, u32[]{:S(2)}) collective-permute-start(f32[24,128]{1,0:T(8,128)S(1)} %get-tuple-element.16), channel_id=1, source_target_pairs={{0,1},{1,2},{2,3},{3,4},{4,5},{5,6},{6,7},{7,0},{8,9},{9,10},{10,1... | collective-permute-start | bytes 36872 | tf_op jit(solution)/shard_map/ppermute | solution.py:319
  44.0 4.0 %collective-permute-start.5 = (f32[24,128]{1,0:T(8,128)S(1)}, f32[24,128]{1,0:T(8,128)S(1)}, u32[]{:S(2)}, u32[]{:S(2)}) collective-permute-start(f32[24,128]{1,0:T(8,128)S(1)} %get-tuple-element.17), channel_id=1, source_target_pairs={{0,7},{1,0},{2,1},{3,2},{4,3},{5,4},{6,5},{7,6},{8,15},{9,8},{10,9... | collective-permute-start | bytes 36872 | tf_op jit(solution)/shard_map/ppermute | solution.py:319
where the time goes:
time: 72.7 us; the launch traced here: 72.3 us
  waiting for transfers between devices  19.6 us (27%)
  Pallas kernels  18 us (25%)
  blocking collectives  16.7 us (23%)
  starting transfers between devices  15.5 us (21%)
  local copies, waits for them, and re-layouts  2.39 us (3%)
    all_to_all x1, blocking collectives, exchange(): lax.all_to_all(slots, ('lat', 'lon'), split_axis=0, concat_axis=0, tiled=...  16.7 us
    all_to_all x1, waiting for transfers between devices, exchange(): lax.all_to_all(slots, ('lat', 'lon'), split_axis=0, concat_axis=0, tiled=...  15.5 us
    ppermute x6, starting transfers between devices, to_next(): return lax.ppermute(array, axis, route)  11.6 us
    pallas_call x1, Pallas kernels, local(): pl.pallas_call(functools.partial(last_kernel, 1, lat_count, lon_count), o...  7.59 us
    pallas_call x1, Pallas kernels, local(): pl.pallas_call(functools.partial(first_kernel, 0, lat_count, lon_count),...  7.45 us
    ppermute x6, waiting for transfers between devices, to_next(): return lax.ppermute(array, axis, route)  4.04 us
    all_to_all x1, starting transfers between devices, exchange(): lax.all_to_all(slots, ('lat', 'lon'), split_axis=0, concat_axis=0, tiled=...  3.94 us
    unnamed x11, local copies, waits for them, and re-layouts  2.39 us
  transfers between devices with their start and end apart: 7, of which 3 were waited for; matrix products, arithmetic and copies ran while one was open for 0% of the time, Pallas kernels for 0%

commit v1 on v0

v1 whole, which is shorter than its diff:
```python
import functools
import jax
import jax.numpy as jnp
from jax import lax
from jax.experimental import pallas as pl
from jax.experimental.pallas import tpu as pltpu
from jax.sharding import PartitionSpec as P

REACH = 2
WIN = 2 * REACH + 1
SUB = 8
LANES = 128
NEAR = (-1, 0, 1)
AT_ROW, AT_COL, AT_OBS = (4, 5, 6)
F32 = jnp.float32
BF16 = jnp.bfloat16


def swap(block, axis, kind, count, wraps):
    route = []
    for place in range(count):
        partner = place + (1 if place % 2 == kind else -1)
        if wraps or 0 <= partner < count:
            route.append((place, partner % count))
    return lax.ppermute(block, axis, route)


def is_even(axis):
    return lax.rem(lax.axis_index(axis), 2) == 0


def start_kernel(
    width, observed, precision, weight, stencil, owned, cells, params_ref, sides_0, sides_1,
    observed_v, precision_v, weight_v, stencil_v, owned_v, left_v, right_v, sems
):
    batches, cols = (observed.shape[0], cells.shape[1])
    pairs = (
        (observed, observed_v),
        (precision, precision_v),
        (weight, weight_v),
        (stencil, stencil_v),
        (owned, owned_v),
        (cells.at[:, pl.ds(0, SUB)], left_v),
        (cells.at[:, pl.ds(cols - SUB, SUB)], right_v),
    )
    copies = [pltpu.make_async_copy(source, target, sems.at[n]) for n, (source, target) in enumerate(pairs)]
    for copy in copies:
        copy.start()
    for copy in copies:
        copy.wait()
    params_ref[...] = jnp.zeros_like(params_ref)
    for b in range(batches):
        root = jnp.sqrt(precision_v[b, 0]) * owned_v[b, 0].astype(F32)
        corner = stencil_v[b, 0, 0, pl.ds(0, 1)].astype(F32)
        row = jnp.floor((corner + 0.5) * (1.0 / width))
        params_ref[b, pl.ds(0, 4), pl.ds(0, SUB)] = weight_v[b, 0, 0] * root
        params_ref[b, pl.ds(AT_ROW, 1), pl.ds(0, SUB)] = row
        params_ref[b, pl.ds(AT_COL, 1), pl.ds(0, SUB)] = corner - row * width
        params_ref[b, pl.ds(AT_OBS, 1), pl.ds(0, SUB)] = observed_v[b, 0] * root
    rows = cells.shape[0]
    even = is_even("lon")
    left, right = (left_v[:, 0, :], right_v[:, SUB - 1, :])
    sides_0[pl.ds(0, rows), :] = jnp.where(even, right, left)
    sides_1[pl.ds(0, rows), :] = jnp.where(even, left, right)
    sides_0[pl.ds(rows, SUB), :] = params_ref[1]
    sides_1[pl.ds(rows, SUB), :] = params_ref[1]


def clear_rim(pad, rows, cols):
    edge = jnp.zeros((2, cols + 2 * SUB, LANES), F32)
    pad[pl.ds(0, 2)] = edge
    pad[pl.ds(rows + 2, 2)] = edge
    side = jnp.zeros((rows, SUB, LANES), F32)
    pad[pl.ds(2, rows), pl.ds(0, SUB)] = side
    pad[pl.ds(2, rows), pl.ds(SUB + cols, SUB)] = side


def share(pad, number, rows, cols, da, dc, o):
    row = number(AT_ROW, o).astype(jnp.int32) - 1 + da * rows
    col = number(AT_COL, o).astype(jnp.int32) - 1 + dc * cols
    row = jnp.clip(row, -2, rows) + 2
    col = jnp.clip(col, -2, cols) + SUB
    terms = [number(k, o) * pad[row + k // 2, pl.ds(col + k % 2, 1), :] for k in range(4)]
    return (terms[0] + terms[1]) + (terms[2] + terms[3])


def own_shift(number):
    sub = lax.broadcasted_iota(jnp.int32, (SUB, LANES), 0)
    shift = jnp.zeros((SUB, LANES), F32)
    for o in range(SUB):
        shift = jnp.where(sub == o, number(AT_OBS, o), shift)
    return shift


def pad_kernel(cells, pad, sem):
    rows, cols = (cells.shape[0], cells.shape[1])
    copy = pltpu.make_async_copy(cells, pad.at[pl.ds(2, rows), pl.ds(SUB, cols)], sem)
    copy.start()
    clear_rim(pad, rows, cols)
    copy.wait()


def column_kernel(mine, sides_0, sides_1, ends_0, ends_1, pad, own_ref, out_0, out_1, block, sides, params, sems):
    rows, cols = (pad.shape[0] - 4, pad.shape[1] - 2 * SUB)
    lon_even, lat_even = (is_even("lon"), is_even("lat"))
    copies = []
    for n, source in enumerate((ends_0, mine.at[0], ends_1)):
        copies.append(pltpu.make_async_copy(source, params.at[n], sems.at[n]))
        copies[-1].start()
    sides[...] = jnp.zeros_like(sides)
    left = jnp.where(lon_even, sides_1[...], sides_0[...])
    right = jnp.where(lon_even, sides_0[...], sides_1[...])
    sides[0, pl.ds(SUB, rows), :] = left[:rows]
    sides[1, pl.ds(SUB, rows), :] = right[:rows]
    lane = lax.broadcasted_iota(jnp.int32, (SUB, LANES), 1)
    packed = jnp.where(lane < SUB, left[rows:], pltpu.roll(mine[1], SUB, 1))
    packed = jnp.where(lane < 2 * SUB, packed, pltpu.roll(right[rows:], 2 * SUB, 1))
    out_0[pl.ds(SUB, SUB), :] = packed
    out_1[pl.ds(SUB, SUB), :] = packed
    for copy in copies:
        copy.wait()
    spots = (jnp.where(lat_even, 2, 0), 1, jnp.where(lat_even, 0, 2))
    for n, da in enumerate(NEAR):
        number = lambda kind, o: params[spots[n], kind, o]
        for o in range(SUB):
            total = share(pad, number, rows, cols, da, 0, o)
            row = number(AT_ROW, o).astype(jnp.int32) - 1 + da * rows
            row = jnp.clip(row, -2, rows) + SUB
            col = number(AT_COL, o).astype(jnp.int32)
            for side, at in enumerate((0, cols)):
                for k in (side, side + 2):
                    weight = jnp.where(col == at, number(k, o), 0.0)
                    total = total + weight * sides[side, pl.ds(row + k // 2, 1), :]
            block[n, pl.ds(o, 1), :] = total
    own_ref[...] = block[1] - own_shift(lambda kind, o: params[1, kind, o])
    out_0[pl.ds(0, SUB), :] = jnp.where(lat_even, block[2], block[0])
    out_1[pl.ds(0, SUB), :] = jnp.where(lat_even, block[0], block[2])


def block_kernel(own, ends_0, ends_1, out_ref):
    part = pl.ds(0, SUB)
    value = own[...] + ends_0[part, :] + ends_1[part, :]
    mean = jnp.mean(value, axis=-1, keepdims=True)
    innov = jnp.broadcast_to(-mean, value.shape)
    block = jnp.concatenate([value - mean, innov], axis=0).astype(BF16)
    out_ref[...] = jnp.broadcast_to(block, out_ref.shape)


def later_kernel(mine, sides_0, sides_1, ends_0, ends_1, pad, out_ref, params, sems):
    rows, cols = (pad.shape[0] - 4, pad.shape[1] - 2 * SUB)
    lon_even, lat_even = (is_even("lon"), is_even("lat"))
    side, end = (pl.ds(rows, SUB), pl.ds(SUB, SUB))
    sources = (sides_0.at[side], mine.at[1], sides_1.at[side], ends_0.at[end], ends_1.at[end])
    copies = []
    for n, source in enumerate(sources):
        copies.append(pltpu.make_async_copy(source, params.at[n], sems.at[n]))
        copies[-1].start()
    for copy in copies:
        copy.wait()
    beside = (jnp.where(lon_even, 2, 0), 1, jnp.where(lon_even, 0, 2))
    above = (jnp.where(lat_even, 4, 3), None, jnp.where(lat_even, 3, 4))
    for n, dc in enumerate(NEAR):
        for m, da in enumerate(NEAR):
            if da == 0:
                number = lambda kind, o: params[beside[n], kind, o]
            else:
                number = lambda kind, o: params[above[m], kind, n * SUB + o]
            for o in range(SUB):
                at = (n * len(NEAR) + m) * SUB + o
                out_ref[pl.ds(at, 1), :] = share(pad, number, rows, cols, da, dc, o)
    out_ref[pl.ds(len(NEAR) ** 2 * SUB, SUB), :] = own_shift(lambda kind, o: params[1, kind, o])


def window_start(lat_count, my_lat):
    return 0 if lat_count <= WIN else jnp.clip(my_lat - REACH, 0, lat_count - WIN)


def row_of(block, j):
    return jnp.broadcast_to(block[j:j + 1, :], (SUB, LANES))


def reciprocal(value):
    guess = pl.reciprocal(value, approx=True)
    return guess * (2.0 - value * guess)


def eliminate(blocks):
    count = len(blocks) - 1
    blocks = list(blocks)
    sub = lax.broadcasted_iota(jnp.int32, (SUB, LANES), 0)
    lane = lax.broadcasted_iota(jnp.int32, (SUB, LANES), 1)
    inverse = []
    for k in range(count):
        here = (lane >= k * SUB) & (lane < (k + 1) * SUB)
        column = [
            [jnp.broadcast_to(blocks[i][:, k * SUB + j:k * SUB + j + 1], (SUB, LANES)) for j in range(SUB)]
            for i in range(k, count + 1)
        ]
        diag = column[0]
        full = jnp.where(here, jnp.where(lane - k * SUB == sub, 1.0, 0.0), blocks[k])
        lower = full
        scale = jnp.zeros((SUB, LANES), F32)
        for j in range(0, SUB, 2):
            a, b, c = (row_of(diag[j], j), row_of(diag[j + 1], j), row_of(diag[j + 1], j + 1))
            det = a * c - b * b
            over_det = reciprocal(det)
            first = jnp.where(sub == j, -c, jnp.where(sub == j + 1, b, diag[j] * c - diag[j + 1] * b))
            second = jnp.where(sub == j, b, jnp.where(sub == j + 1, -a, diag[j + 1] * a - diag[j] * b))
            first, second = (first * over_det, second * over_det)
            other = (sub != j) & (sub != j + 1)
            for n in range(j + 2, SUB):
                diag[n] = jnp.where(other, diag[n], 0.0) - first * row_of(diag[n], j) - second * row_of(diag[n], j + 1)
            full = jnp.where(other, full, 0.0) - first * row_of(full, j) - second * row_of(full, j + 1)
            over_a = reciprocal(a)
            top, bottom = (row_of(lower, j), row_of(lower, j + 1))
            below = sub > j + 1
            lower = lower - jnp.where(sub == j + 1, b * over_a, jnp.where(below, first, 0.0)) * top
            lower = lower - jnp.where(below, second, 0.0) * bottom
            scale = jnp.where(sub == j, lax.rsqrt(a), jnp.where(sub == j + 1, lax.rsqrt(det * over_a), scale))
        inverse.append(jnp.where(lane < (k + 1) * SUB, lower * scale, 0.0))
        pivot = [row_of(full, j) for j in range(SUB)]
        for i in range(k + 1, count + 1):
            terms = [column[i - k][j] * pivot[j] for j in range(SUB)]
            while len(terms) > 1:
                terms = [terms[n] + terms[n + 1] for n in range(0, len(terms), 2)]
            blocks[i] = jnp.where(here, 0.0, blocks[i]) - terms[0]
    return inverse, blocks[count][:1]


def batch_map(batch, lat_count, near_ref, pattern_ref):
    lon_count = pattern_ref.shape[-1]
    held = min(WIN, lat_count)
    my_lat = lax.axis_index("lat")
    start = window_start(lat_count, my_lat)
    marks = []
    for j in range(held):
        offset = start + j - my_lat + REACH
        inside = (offset >= 0) & (offset < WIN)
        offset = jnp.clip(offset, 0, WIN - 1)
        for e in range(lon_count):
            mark = jnp.where(inside, pattern_ref[batch, 0, 0, offset, e], 0).astype(F32)
            marks.append(jnp.full((SUB, LANES), mark))
    marks = jnp.concatenate(marks, axis=0)
    near = near_ref[...].astype(F32)
    scaled = near[:, :SUB].reshape(-1, LANES)
    innov = near[:, SUB:].reshape(-1, LANES)
    weighted = scaled * marks
    scaled = scaled.astype(BF16)
    proj = jnp.sum((weighted * innov).reshape(-1, SUB, LANES), axis=0)
    proj = jnp.sum(proj, axis=0, keepdims=True)
    gram = lax.dot_general(
        weighted.astype(BF16), scaled, (((0,), (0,)), ((), ())), preferred_element_type=F32
    )
    sub = lax.broadcasted_iota(jnp.int32, (SUB, LANES), 0)
    lane = lax.broadcasted_iota(jnp.int32, (SUB, LANES), 1)
    members = LANES
    blocks = []
    for k in range(members // SUB):
        block = gram[k * SUB:(k + 1) * SUB, :]
        blocks.append(block + jnp.where(lane - k * SUB == sub, members - 1.0, 0.0))
    blocks.append(jnp.broadcast_to(proj, (SUB, LANES)))
    inverse, weights = eliminate(blocks)
    flipped = jnp.concatenate(inverse, axis=0) * (members - 1.0) ** 0.5 - weights
    return flipped - jnp.mean(flipped, axis=-1, keepdims=True) + 1.0 / members


def exact_dot(a, b, contract_b):
    return lax.dot_general(
        a, b, (((1,), (contract_b,)), ((), ())), precision=lax.Precision.HIGHEST, preferred_element_type=F32
    )


def first_kernel(batch, lat_count, near_ref, pattern_ref, later, mid_ref, out_0, out_1, map_ref):
    flipped = batch_map(batch, lat_count, near_ref, pattern_ref)
    map_ref[...] = flipped
    size = len(NEAR) * SUB
    moved = exact_dot(later[pl.ds(0, len(NEAR) * size), :], flipped, 1)
    left, right = (moved[:size], moved[2 * size:])
    even = is_even("lon")
    out_0[...] = jnp.where(even, right, left)
    out_1[...] = jnp.where(even, left, right)
    mid_ref[...] = moved[size:2 * size]
    own = pl.ds(SUB, SUB)
    mid_ref[own, :] = mid_ref[own, :] - later[pl.ds(len(NEAR) * size, SUB), :]


def meet_kernel(mid, sides_0, sides_1, own_ref, out_0, out_1):
    total = mid[...] + sides_0[...] + sides_1[...]
    above, own_ref[...], below = (total[:SUB], total[SUB:2 * SUB], total[2 * SUB:])
    even = is_even("lat")
    out_0[...] = jnp.where(even, below, above)
    out_1[...] = jnp.where(even, above, below)


def last_kernel(
    batch, lat_count, near_ref, pattern_ref, map_ref, cells_ref, out_ref, cells, result, cell_sem, out_sem
):
    parts = out_sem.shape[0]
    rows = cells.shape[0] // parts
    copy = pltpu.make_async_copy(cells_ref, cells, cell_sem)
    copy.start()
    flipped = exact_dot(batch_map(batch, lat_count, near_ref, pattern_ref), map_ref[...], 0)
    high = flipped.astype(BF16)
    low = (flipped - high.astype(F32)).astype(BF16)
    right = jnp.concatenate(
        [jnp.concatenate([high, high], axis=1), jnp.concatenate([low, jnp.zeros_like(low)], axis=1)], axis=0
    )
    copy.wait()
    copies = []
    for n in range(parts):
        part = pl.ds(n * rows, rows)
        value = cells[part, :]
        upper = value.astype(BF16)
        rest = (value - upper.astype(F32)).astype(BF16)
        both = lax.dot_general(
            jnp.concatenate([upper, rest], axis=1), right, (((1,), (1,)), ((), ())), preferred_element_type=F32
        )
        result[part, :] = both[:, :LANES] + both[:, LANES:]
        copies.append(pltpu.make_async_copy(result.at[part], out_ref.at[part], out_sem.at[n]))
        copies[-1].start()
    for out_copy in copies:
        out_copy.wait()


def window(tiles, lat_count, lon_count):
    held = min(WIN, lat_count)
    if held == lat_count:
        return tiles
    start = jnp.clip(lax.axis_index("lat") - REACH, 0, lat_count - held)
    return lax.dynamic_slice_in_dim(tiles, start * lon_count, held * lon_count, axis=0)


def local(ensemble, observed, precision, interp_weight, stencil, owned, pattern):
    rows, cols, members = ensemble.shape
    batches = observed.shape[0]
    lat_count, lon_count = (lax.axis_size("lat"), lax.axis_size("lon"))
    tiles = lat_count * lon_count
    column = len(NEAR) * SUB
    vmem = pl.BlockSpec(memory_space=pltpu.VMEM)
    smem = pl.BlockSpec(memory_space=pltpu.SMEM)
    anywhere = pl.BlockSpec(memory_space=pl.ANY)
    hbm = pl.BlockSpec(memory_space=pltpu.HBM)
    megabyte = 1024 * 1024

    def shape(*dims, dtype=F32):
        return jax.ShapeDtypeStruct(dims, dtype)

    def call(kernel, name, specs, out_shape, scratch, *operands, out_specs=None, limit=48):
        return pl.pallas_call(
            kernel,
            out_shape=out_shape,
            in_specs=specs,
            out_specs=out_specs or jax.tree.map(lambda _: vmem, out_shape),
            scratch_shapes=scratch,
            compiler_params=pltpu.CompilerParams(vmem_limit_bytes=limit * megabyte),
            name=name,
        )(*operands)

    def trade(blocks, axis):
        count, wraps = ((lon_count, True) if axis == "lon" else (lat_count, False))
        second = swap(blocks[1], axis, 1, count, wraps)
        first = swap(blocks[0], axis, 0, count, wraps)
        return (first, second)

    def gathered(own, ends):
        block = shape(tiles, 2 * SUB, members, dtype=BF16)
        blocks = call(block_kernel, "own_block", [vmem] * 3, block, [], own, *ends)
        blocks = lax.all_to_all(blocks, ("lat", "lon"), split_axis=0, concat_axis=0, tiled=True)
        return window(blocks, lat_count, lon_count)

    small = (observed, precision, interp_weight, stencil, owned)
    side = shape(rows + SUB, members)
    mine, *sides = call(
        functools.partial(start_kernel, cols + 2),
        "start",
        [hbm] * 6,
        (shape(batches, SUB, LANES), side, side),
        [pltpu.VMEM(array.shape, array.dtype) for array in small]
        + [pltpu.VMEM((rows, SUB, members), F32)] * 2
        + [pltpu.SemaphoreType.DMA((7,))],
        *small,
        ensemble,
        limit=63,
    )
    sides = trade(sides, "lon")
    ends = trade((mine[0], mine[0]), "lat")
    padded = shape(rows + 4, cols + 2 * SUB, members)
    pad = call(pad_kernel, "pad", [hbm], padded, [pltpu.SemaphoreType.DMA], ensemble)
    end = shape(2 * SUB, members)
    own, *ends = call(
        column_kernel,
        "column_shares",
        [vmem] * 6,
        (shape(SUB, members), end, end),
        [
            pltpu.VMEM((3, SUB, members), F32),
            pltpu.VMEM((2, rows + 2 * SUB, members), F32),
            pltpu.SMEM((3, SUB, LANES), F32),
            pltpu.SemaphoreType.DMA((3,)),
        ],
        mine,
        *sides,
        *ends,
        pad,
    )
    ends = trade(ends, "lat")
    near = gathered(own, ends)
    later = call(
        later_kernel,
        "later_shares",
        [vmem] * 6,
        shape(len(NEAR) * column + SUB, members),
        [pltpu.SMEM((5, SUB, LANES), F32), pltpu.SemaphoreType.DMA((5,))],
        mine,
        *sides,
        *ends,
        pad,
    )
    part = shape(column, members)
    mid, first, second, first_map = call(
        functools.partial(first_kernel, 0, lat_count),
        "first_batch",
        [vmem, smem, vmem],
        (part, part, part, shape(members, members)),
        [],
        near,
        pattern,
        later,
    )
    sides = trade((first, second), "lon")
    block = shape(SUB, members)
    own, *ends = call(meet_kernel, "meet", [vmem] * 3, (block, block, block), [], mid, *sides)
    near = gathered(own, trade(ends, "lat"))
    parts = 8
    result = call(
        functools.partial(last_kernel, 1, lat_count),
        "second_batch",
        [vmem, smem, vmem, anywhere],
        shape(rows * cols, members),
        [
            pltpu.VMEM((rows * cols, members), F32),
            pltpu.VMEM((rows * cols, members), F32),
            pltpu.SemaphoreType.DMA,
            pltpu.SemaphoreType.DMA((parts,)),
        ],
        near,
        pattern,
        first_map,
        ensemble.reshape(rows * cols, members),
        out_specs=anywhere,
    )
    return result.reshape(rows, cols, members)


def solution(mesh):
    placed = (
        P("lat", "lon", None),
        P(None, "lat", "lon", None),
        P(None, "lat", "lon", None),
        P(None, "lat", "lon", None, None),
        P(None, "lat", "lon", None, None),
        P(None, "lat", "lon", None),
        P(None, "lat", "lon", None, None),
    )
    return jax.shard_map(
        local, mesh=mesh, in_specs=placed, out_specs=P("lat", "lon", None), check_vma=False
    )
```

time: 72.7 us -> 67.8 us (0.933)
  waiting for transfers between devices: 19.6 us -> 13.3 us
  blocking collectives: 16.7 us -> 12.3 us
  starting transfers between devices: 15.5 us -> 19.1 us
  local copies, waits for them, and re-layouts: 2.39 us -> 3.93 us
    all_to_all x1, waiting for transfers between devices: 15.5 us -> 6.61 us  [gathered(): lax.all_to_all(blocks, ('lat', 'lon'), split_axis=0, concat_axis=0, tiled...]
    all_to_all x1, blocking collectives: 16.7 us -> 12.3 us  [gathered(): lax.all_to_all(blocks, ('lat', 'lon'), split_axis=0, concat_axis=0, tiled...]
    ppermute x6 -> x10, waiting for transfers between devices: 4.04 us -> 6.67 us  [swap(): return lax.ppermute(block, axis, route)]
    ppermute x6 -> x10, starting transfers between devices: 11.6 us -> 13.6 us  [swap(): return lax.ppermute(block, axis, route)]
    all_to_all x1, starting transfers between devices: 3.94 us -> 5.45 us  [gathered(): lax.all_to_all(blocks, ('lat', 'lon'), split_axis=0, concat_axis=0, tiled...]
    unnamed x11 -> x9, local copies, waits for them, and re-layouts: 2.39 us -> 3.19 us
    squeeze x0 -> x1, local copies, waits for them, and re-layouts: none -> 0.74 us  [local(): ends = trade((mine[0], mine[0]), 'lat')]
    pallas_call x6 -> x9, Pallas kernels: 18 us -> 18.7 us  [call(): pl.pallas_call(kernel, out_shape=out_shape, in_specs=specs, out_specs=out...]
  transfers between devices with their start and end apart: 7 -> 11, of which waited for: 3 -> 5; matrix products, arithmetic and copies ran while one was open for 0% -> 1% of each run, Pallas kernels for 0% -> 3%
where the time goes in v1:
time: 67.8 us; the launch traced here: 67.4 us
  starting transfers between devices  19.1 us (28%)
  Pallas kernels  18.7 us (28%)
  waiting for transfers between devices  13.3 us (20%)
  blocking collectives  12.3 us (18%)
  local copies, waits for them, and re-layouts  3.93 us (6%)
    pallas_call x9, Pallas kernels, call(): pl.pallas_call(kernel, out_shape=out_shape, in_specs=specs, out_specs=out...  18.7 us
    ppermute x10, starting transfers between devices, swap(): return lax.ppermute(block, axis, route)  13.6 us
    all_to_all x1, blocking collectives, gathered(): lax.all_to_all(blocks, ('lat', 'lon'), split_axis=0, concat_axis=0, tiled...  12.3 us
    ppermute x10, waiting for transfers between devices, swap(): return lax.ppermute(block, axis, route)  6.67 us
    all_to_all x1, waiting for transfers between devices, gathered(): lax.all_to_all(blocks, ('lat', 'lon'), split_axis=0, concat_axis=0, tiled...  6.61 us
    all_to_all x1, starting transfers between devices, gathered(): lax.all_to_all(blocks, ('lat', 'lon'), split_axis=0, concat_axis=0, tiled...  5.45 us
    unnamed x9, local copies, waits for them, and re-layouts  3.19 us
  transfers between devices with their start and end apart: 11, of which 5 were waited for; matrix products, arithmetic and copies ran while one was open for 1% of the time, Pallas kernels for 3%

profile of v1, /device:TPU:0, one launch (start us, length us, event | category | flops | bytes accessed | tf_op | source)
XLA Modules:
  0.0 67.4 jit_solution(12064586191828018725)
XLA Ops:
  0.0 1.8 %start.1 = (f32[2,8,128]{2,1,0:T(8,128)}, f32[40,128]{1,0:T(8,128)}, f32[40,128]{1,0:T(8,128)}) custom-call(f32[2,1,1,8]{3,2,1,0:T(1,128)} %observed.1, f32[2,1,1,8]{3,2,1,0:T(1,128)} %precision.1, f32[2,1,1,4,8]{4,3,2,1,0:T(4,128)} %weight.1, s32[2,1,1,4,8]{4,3,2,1,0:T(4,128)} %stencil.1, s32[2,1,1,8]{3,2,1,0:T(1,128)} %owned.1, f32[32,128,128]{2,1,0:T(8,128)} %cells.3), custom_call_target="tpu_custom_call" | custom-call | tf_op jit(solution)/shard_map/start/pallas_call | solution.py:349
  1.8 0.5 collective-permute-start
  2.3 3.6 %collective-permute-start.1 = (f32[40,128]{1,0:T(8,128)}, f32[40,128]{1,0:T(8,128)S(1)}, u32[]{:S(2)}, u32[]{:S(2)}) collective-permute-start(f32[40,128]{1,0:T(8,128)} %get-tuple-element.20), channel_id=1, source_target_pairs={{0,7},{1,2},{2,1},{3,4},{4,3},{5,6},{6,5},{7,0},{8,15},{9,10},{10,... | collective-permute-start | bytes 61448 | tf_op jit(solution)/shard_map/ppermute | solution.py:25
  5.8 0.0 copy-start.2
  5.8 0.7 %slice_bitcast_fusion = f32[8,128]{1,0:T(8,128)S(1)} fusion(f32[2,8,128]{2,1,0:T(8,128)} %get-tuple-element.18.mine), kind=kLoop, calls=%fused_computation | loop fusion | bytes 8192 | tf_op jit(solution)/shard_map/squeeze | solution.py:386
  6.6 1.6 %collective-permute-start.2 = (f32[8,128]{1,0:T(8,128)S(1)}, f32[8,128]{1,0:T(8,128)S(1)}, u32[]{:S(2)}, u32[]{:S(2)}) collective-permute-start(f32[8,128]{1,0:T(8,128)S(1)} %slice_bitcast_fusion), channel_id=1, source_target_pairs={{0,8},{8,0},{16,24},{24,16},{1,9},{9,1},{17,25},{25,17},{2,10},{10... | collective-permute-start | bytes 12296 | tf_op jit(solution)/shard_map/ppermute | solution.py:25
  8.2 0.6 collective-permute-start.3
  8.8 0.0 copy-start
  8.8 1.6 %copy-done = f32[32,128,128]{2,1,0:T(8,128)S(1)} copy-done((f32[32,128,128]{2,1,0:T(8,128)S(1)}, f32[32,128,128]{2,1,0:T(8,128)}, u32[]{:S(2)}) %copy-start) | copy-done | bytes 2097176
  10.4 0.2 pad.1
  10.6 0.0 copy-start.3
  10.6 0.0 collective-permute-done.2.ends_0
  10.7 0.0 collective-permute-done.3.ends_1
  10.7 0.0 collective-permute-done.sides_0
  10.7 0.0 collective-permute-done.1.sides_1
  10.7 0.0 copy-done.2
  10.7 1.0 %column_shares.1 = (f32[8,128]{1,0:T(8,128)S(1)}, f32[16,128]{1,0:T(8,128)S(1)}, f32[16,128]{1,0:T(8,128)S(1)}) custom-call(f32[2,8,128]{2,1,0:T(8,128)S(1)} %copy-done.2, f32[40,128]{1,0:T(8,128)S(1)} %collective-permute-done.sides_0, f32[40,128]{1,0:T(8,128)S(1)} %collective-permute-done.1.sides_1, f32[8,128]{1,0:T(8,128)S(1)} %collective-permute-done.2.ends_0, ...), custom_call_target="tpu_custom_call" | custom-call | tf_op jit(solution)/shard_map/column_shares/pallas_call | solution.py:349
  11.7 4.5 %collective-permute-start.4 = (f32[16,128]{1,0:T(8,128)S(1)}, f32[16,128]{1,0:T(8,128)S(1)}, u32[]{:S(2)}, u32[]{:S(2)}) collective-permute-start(f32[16,128]{1,0:T(8,128)S(1)} %get-tuple-element.22), channel_id=1, source_target_pairs={{0,8},{8,0},{16,24},{24,16},{1,9},{9,1},{17,25},{25,17},{2,10},{10... | collective-permute-start | bytes 24584 | tf_op jit(solution)/shard_map/ppermute | solution.py:25
  16.2 0.6 collective-permute-start.5
  16.9 1.0 %collective-permute-done.4.ends_0 = f32[16,128]{1,0:T(8,128)S(1)} collective-permute-done((f32[16,128]{1,0:T(8,128)S(1)}, f32[16,128]{1,0:T(8,128)S(1)}, u32[]{:S(2)}, u32[]{:S(2)}) %collective-permute-start.4) | collective-permute-done | bytes 8224 | tf_op jit(solution)/shard_map/ppermute | solution.py:25
  17.8 0.0 collective-permute-done.5.ends_1
  17.8 0.7 %own_block.2 = bf16[32,16,128]{2,1,0:T(8,128)(2,1)} custom-call(f32[8,128]{1,0:T(8,128)S(1)} %get-tuple-element.21.own, f32[16,128]{1,0:T(8,128)S(1)} %collective-permute-done.4.ends_0, f32[16,128]{1,0:T(8,128)S(1)} %collective-permute-done.5.ends_1), custom_call_target="tpu_custom_call" | custom-call | tf_op jit(solution)/shard_map/own_block/pallas_call | solution.py:349
  18.6 5.5 %all-to-all-start = ((bf16[32,16,128]{2,1,0:T(8,128)(2,1)}), bf16[32,16,128]{2,1,0:T(8,128)(2,1)S(1)}, u32[]{:S(2)}, u32[]{:S(2)}) async-start(bf16[32,16,128]{2,1,0:T(8,128)(2,1)} %own_block.2), calls=%async_computation | async-start | bytes 262144 | tf_op jit(solution)/shard_map/all_to_all | solution.py:368
  24.0 0.0 copy-done.3
  24.1 1.6 %later_shares.1.later = f32[80,128]{1,0:T(8,128)S(1)} custom-call(f32[2,8,128]{2,1,0:T(8,128)S(1)} %copy-done.2, f32[40,128]{1,0:T(8,128)S(1)} %collective-permute-done.sides_0, f32[40,128]{1,0:T(8,128)S(1)} %collective-permute-done.1.sides_1, f32[16,128]{1,0:T(8,128)S(1)} %collective-permute-done.4.ends_0, f32[16,128]{1,0:T(8,128)S(1)} %collective-permute-done.5.ends_1, ...), custom_call_target="tpu_custom_call" | custom-call | tf_op jit(solution)/shard_map/later_shares/pallas_call | solution.py:349
  25.7 6.6 %all-to-all-done.near_ref = bf16[32,16,128]{2,1,0:T(8,128)(2,1)S(1)} async-done(((bf16[32,16,128]{2,1,0:T(8,128)(2,1)}), bf16[32,16,128]{2,1,0:T(8,128)(2,1)S(1)}, u32[]{:S(2)}, u32[]{:S(2)}) %all-to-all-start) | async-done | bytes 131104 | tf_op jit(solution)/shard_map/all_to_all | solution.py:368
  32.3 5.7 %first_batch.1 = (f32[24,128]{1,0:T(8,128)S(1)}, f32[24,128]{1,0:T(8,128)S(1)}, f32[24,128]{1,0:T(8,128)S(1)}, f32[128,128]{1,0:T(8,128)S(1)}) custom-call(bf16[32,16,128]{2,1,0:T(8,128)(2,1)S(1)} %all-to-all-done.near_ref, s32[2,1,1,5,8]{4,3,2,1,0:T(8,128)S(1)} %copy.8.pattern_ref, f32[80,128]{1,0:T(8,128)S(1)} %later_shares.1.later), custom_call_target="tpu_custom_call" | custom-call | tf_op jit(solution)/shard_map/first_batch/pallas_call | solution.py:349
  38.0 0.3 collective-permute-start.6
  38.3 0.8 %collective-permute-start.7 = (f32[24,128]{1,0:T(8,128)S(1)}, f32[24,128]{1,0:T(8,128)S(1)}, u32[]{:S(2)}, u32[]{:S(2)}) collective-permute-start(f32[24,128]{1,0:T(8,128)S(1)} %get-tuple-element.26), channel_id=1, source_target_pairs={{0,7},{1,2},{2,1},{3,4},{4,3},{5,6},{6,5},{7,0},{8,15},{9,10},{10,... | collective-permute-start | bytes 36872 | tf_op jit(solution)/shard_map/ppermute | solution.py:25
  39.0 0.2 collective-permute-done.6.sides_0
  39.2 3.1 %collective-permute-done.7.sides_1 = f32[24,128]{1,0:T(8,128)S(1)} collective-permute-done((f32[24,128]{1,0:T(8,128)S(1)}, f32[24,128]{1,0:T(8,128)S(1)}, u32[]{:S(2)}, u32[]{:S(2)}) %collective-permute-start.7) | collective-permute-done | bytes 12320 | tf_op jit(solution)/shard_map/ppermute | solution.py:25
  42.3 0.5 collective-permute-start.8
  42.8 0.6 collective-permute-start.9
  43.5 2.4 %collective-permute-done.8.ends_0 = f32[8,128]{1,0:T(8,128)S(1)} collective-permute-done((f32[8,128]{1,0:T(8,128)S(1)}, f32[8,128]{1,0:T(8,128)S(1)}, u32[]{:S(2)}, u32[]{:S(2)}) %collective-permute-start.8) | collective-permute-done | bytes 4128 | tf_op jit(solution)/shard_map/ppermute | solution.py:25
  45.9 0.0 collective-permute-done.9.ends_1
  45.9 0.1 own_block.3
  46.0 12.3 %all_to_all.10.near_ref = bf16[32,16,128]{2,1,0:T(8,128)(2,1)S(1)} all-to-all(bf16[32,16,128]{2,1,0:T(8,128)(2,1)S(1)} %own_block.3), channel_id=1, replica_groups=mesh['lat'=4,'lon'=8] {'lat','lon'}, dimensions={0} | all-to-all | bytes 262144 | tf_op jit(solution)/shard_map/all_to_all | solution.py:368
  58.3 0.0 copy-start.1
  58.3 1.6 %copy-done.1 = f32[32,128,128]{2,1,0:T(8,128)S(1)} copy-done((f32[32,128,128]{2,1,0:T(8,128)S(1)}, f32[32,128,128]{2,1,0:T(8,128)}, u32[]{:S(2)}) %copy-start.1) | copy-done | bytes 2097176
  59.9 7.5 %second_batch.1 = f32[4096,128]{1,0:T(8,128)} custom-call(bf16[32,16,128]{2,1,0:T(8,128)(2,1)S(1)} %all_to_all.10.near_ref, s32[2,1,1,5,8]{4,3,2,1,0:T(8,128)S(1)} %copy.8.pattern_ref, f32[128,128]{1,0:T(8,128)S(1)} %get-tuple-element.30.map_ref, f32[4096,128]{1,0:T(8,128)S(1)} %bitcast.4), custom_call_target="tpu_custom_call" | custom-call | tf_op jit(solution)/shard_map/second_batch/pallas_call | solution.py:349
  (2 shorter events, 0.0 us)
Async XLA Ops:
  1.8 8.9 %collective-permute-start = (f32[40,128]{1,0:T(8,128)}, f32[40,128]{1,0:T(8,128)S(1)}, u32[]{:S(2)}, u32[]{:S(2)}) collective-permute-start(f32[40,128]{1,0:T(8,128)} %get-tuple-element.19), channel_id=1, source_target_pairs={{0,1},{1,0},{2,3},{3,2},{4,5},{5,4},{6,7},{7,6},{8,9},{9,8},{10,11... | collective-permute-start | bytes 61448 | tf_op jit(solution)/shard_map/ppermute | solution.py:25
  2.3 8.4 %collective-permute-start.1 = (f32[40,128]{1,0:T(8,128)}, f32[40,128]{1,0:T(8,128)S(1)}, u32[]{:S(2)}, u32[]{:S(2)}) collective-permute-start(f32[40,128]{1,0:T(8,128)} %get-tuple-element.20), channel_id=1, source_target_pairs={{0,7},{1,2},{2,1},{3,4},{4,3},{5,6},{6,5},{7,0},{8,15},{9,10},{10,... | collective-permute-start | bytes 61448 | tf_op jit(solution)/shard_map/ppermute | solution.py:25
  5.8 4.8 %copy-start.2 = (f32[2,8,128]{2,1,0:T(8,128)S(1)}, f32[2,8,128]{2,1,0:T(8,128)}, u32[]{:S(2)}) copy-start(f32[2,8,128]{2,1,0:T(8,128)} %get-tuple-element.18.mine) | copy-start | bytes 24580
  6.6 4.1 %collective-permute-start.2 = (f32[8,128]{1,0:T(8,128)S(1)}, f32[8,128]{1,0:T(8,128)S(1)}, u32[]{:S(2)}, u32[]{:S(2)}) collective-permute-start(f32[8,128]{1,0:T(8,128)S(1)} %slice_bitcast_fusion), channel_id=1, source_target_pairs={{0,8},{8,0},{16,24},{24,16},{1,9},{9,1},{17,25},{25,17},{2,10},{10... | collective-permute-start | bytes 12296 | tf_op jit(solution)/shard_map/ppermute | solution.py:25
  8.2 2.5 %collective-permute-start.3 = (f32[8,128]{1,0:T(8,128)S(1)}, f32[8,128]{1,0:T(8,128)S(1)}, u32[]{:S(2)}, u32[]{:S(2)}) collective-permute-start(f32[8,128]{1,0:T(8,128)S(1)} %slice_bitcast_fusion), channel_id=1, source_target_pairs={{8,16},{16,8},{9,17},{17,9},{10,18},{18,10},{11,19},{19,11},{12,20... | collective-permute-start | bytes 12296 | tf_op jit(solution)/shard_map/ppermute | solution.py:25
  8.8 1.6 %copy-start = (f32[32,128,128]{2,1,0:T(8,128)S(1)}, f32[32,128,128]{2,1,0:T(8,128)}, u32[]{:S(2)}) copy-start(f32[32,128,128]{2,1,0:T(8,128)} %cells.3) | copy-start | bytes 6291460
  10.6 13.4 %copy-start.3 = (s32[2,1,1,5,8]{4,2,3,1,0:T(1,128)S(1)}, s32[2,1,1,5,8]{4,2,3,1,0:T(1,128)}, u32[]{:S(2)}) copy-start(s32[2,1,1,5,8]{4,2,3,1,0:T(1,128)} %param.13) | copy-start | bytes 964
  11.7 6.1 %collective-permute-start.4 = (f32[16,128]{1,0:T(8,128)S(1)}, f32[16,128]{1,0:T(8,128)S(1)}, u32[]{:S(2)}, u32[]{:S(2)}) collective-permute-start(f32[16,128]{1,0:T(8,128)S(1)} %get-tuple-element.22), channel_id=1, source_target_pairs={{0,8},{8,0},{16,24},{24,16},{1,9},{9,1},{17,25},{25,17},{2,10},{10... | collective-permute-start | bytes 24584 | tf_op jit(solution)/shard_map/ppermute | solution.py:25
  16.2 1.6 %collective-permute-start.5 = (f32[16,128]{1,0:T(8,128)S(1)}, f32[16,128]{1,0:T(8,128)S(1)}, u32[]{:S(2)}, u32[]{:S(2)}) collective-permute-start(f32[16,128]{1,0:T(8,128)S(1)} %get-tuple-element.23), channel_id=1, source_target_pairs={{8,16},{16,8},{9,17},{17,9},{10,18},{18,10},{11,19},{19,11},{12,20... | collective-permute-start | bytes 24584 | tf_op jit(solution)/shard_map/ppermute | solution.py:25
  18.6 13.7 %all-to-all-start = ((bf16[32,16,128]{2,1,0:T(8,128)(2,1)}), bf16[32,16,128]{2,1,0:T(8,128)(2,1)S(1)}, u32[]{:S(2)}, u32[]{:S(2)}) async-start(bf16[32,16,128]{2,1,0:T(8,128)(2,1)} %own_block.2), calls=%async_computation | async-start | bytes 262144 | tf_op jit(solution)/shard_map/all_to_all | solution.py:368
  38.0 1.2 %collective-permute-start.6 = (f32[24,128]{1,0:T(8,128)S(1)}, f32[24,128]{1,0:T(8,128)S(1)}, u32[]{:S(2)}, u32[]{:S(2)}) collective-permute-start(f32[24,128]{1,0:T(8,128)S(1)} %get-tuple-element.25), channel_id=1, source_target_pairs={{0,1},{1,0},{2,3},{3,2},{4,5},{5,4},{6,7},{7,6},{8,9},{9,8},{10,11... | collective-permute-start | bytes 36872 | tf_op jit(solution)/shard_map/ppermute | solution.py:25
  38.3 4.0 %collective-permute-start.7 = (f32[24,128]{1,0:T(8,128)S(1)}, f32[24,128]{1,0:T(8,128)S(1)}, u32[]{:S(2)}, u32[]{:S(2)}) collective-permute-start(f32[24,128]{1,0:T(8,128)S(1)} %get-tuple-element.26), channel_id=1, source_target_pairs={{0,7},{1,2},{2,1},{3,4},{4,3},{5,6},{6,5},{7,0},{8,15},{9,10},{10,... | collective-permute-start | bytes 36872 | tf_op jit(solution)/shard_map/ppermute | solution.py:25
  42.3 3.6 %collective-permute-start.8 = (f32[8,128]{1,0:T(8,128)S(1)}, f32[8,128]{1,0:T(8,128)S(1)}, u32[]{:S(2)}, u32[]{:S(2)}) collective-permute-start(f32[8,128]{1,0:T(8,128)S(1)} %get-tuple-element.28), channel_id=1, source_target_pairs={{0,8},{8,0},{16,24},{24,16},{1,9},{9,1},{17,25},{25,17},{2,10},{10... | collective-permute-start | bytes 12296 | tf_op jit(solution)/shard_map/ppermute | solution.py:25
  42.8 3.1 %collective-permute-start.9 = (f32[8,128]{1,0:T(8,128)S(1)}, f32[8,128]{1,0:T(8,128)S(1)}, u32[]{:S(2)}, u32[]{:S(2)}) collective-permute-start(f32[8,128]{1,0:T(8,128)S(1)} %get-tuple-element.29), channel_id=1, source_target_pairs={{8,16},{16,8},{9,17},{17,9},{10,18},{18,10},{11,19},{19,11},{12,20... | collective-permute-start | bytes 12296 | tf_op jit(solution)/shard_map/ppermute | solution.py:25
  58.3 1.6 %copy-start.1 = (f32[32,128,128]{2,1,0:T(8,128)S(1)}, f32[32,128,128]{2,1,0:T(8,128)}, u32[]{:S(2)}) copy-start(f32[32,128,128]{2,1,0:T(8,128)} %cells.3) | copy-start | bytes 6291460

commit v2 on v1

v2 whole, which is shorter than its diff:
```python
import functools
import jax
import jax.numpy as jnp
from jax import lax
from jax.experimental import pallas as pl
from jax.experimental.pallas import tpu as pltpu
from jax.sharding import PartitionSpec as P

REACH = 2
WIN = 2 * REACH + 1
SUB = 8
LANES = 128
NEAR = (-1, 0, 1)
AT_ROW, AT_COL, AT_OBS = (4, 5, 6)
MEAN_LANES = 32
F32 = jnp.float32
BF16 = jnp.bfloat16


def swap(block, axis, kind, count, wraps):
    route = []
    for place in range(count):
        partner = place + (1 if place % 2 == kind else -1)
        if wraps or 0 <= partner < count:
            route.append((place, partner % count))
    return lax.ppermute(block, axis, route)


def is_even(axis):
    return lax.rem(lax.axis_index(axis), 2) == 0


def start_kernel(
    width, observed, precision, weight, stencil, owned, pattern, cells, params_ref, marks_ref, sides_0, sides_1,
    observed_v, precision_v, weight_v, stencil_v, owned_v, pattern_v, left_v, right_v, sems
):
    batches, cols = (observed.shape[0], cells.shape[1])
    pairs = (
        (observed, observed_v),
        (precision, precision_v),
        (weight, weight_v),
        (stencil, stencil_v),
        (owned, owned_v),
        (pattern, pattern_v),
        (cells.at[:, pl.ds(0, SUB)], left_v),
        (cells.at[:, pl.ds(cols - SUB, SUB)], right_v),
    )
    copies = [pltpu.make_async_copy(source, target, sems.at[n]) for n, (source, target) in enumerate(pairs)]
    for copy in copies:
        copy.start()
    for copy in copies:
        copy.wait()
    params_ref[...] = jnp.zeros_like(params_ref)
    marks_ref[...] = jnp.zeros_like(marks_ref)
    for b in range(batches):
        marks_ref[b, pl.ds(0, WIN), pl.ds(0, pattern.shape[-1])] = pattern_v[b, :, 0, :].astype(F32)
        root = jnp.sqrt(precision_v[b, 0]) * owned_v[b, 0].astype(F32)
        corner = stencil_v[b, 0, 0, pl.ds(0, 1)].astype(F32)
        row = jnp.floor((corner + 0.5) * (1.0 / width))
        params_ref[b, pl.ds(0, 4), pl.ds(0, SUB)] = weight_v[b, 0, 0] * root
        params_ref[b, pl.ds(AT_ROW, 1), pl.ds(0, SUB)] = row
        params_ref[b, pl.ds(AT_COL, 1), pl.ds(0, SUB)] = corner - row * width
        params_ref[b, pl.ds(AT_OBS, 1), pl.ds(0, SUB)] = observed_v[b, 0] * root
    rows = cells.shape[0]
    even = is_even("lon")
    left, right = (left_v[:, 0, :], right_v[:, SUB - 1, :])
    sides_0[pl.ds(0, rows), :] = jnp.where(even, right, left)
    sides_1[pl.ds(0, rows), :] = jnp.where(even, left, right)
    sides_0[pl.ds(rows, SUB), :] = marks_ref[0]
    sides_1[pl.ds(rows, SUB), :] = marks_ref[0]


def clear_rim(pad, rows, cols):
    edge = jnp.zeros((2, cols + 2 * SUB, LANES), F32)
    pad[pl.ds(0, 2)] = edge
    pad[pl.ds(rows + 2, 2)] = edge
    side = jnp.zeros((rows, SUB, LANES), F32)
    pad[pl.ds(2, rows), pl.ds(0, SUB)] = side
    pad[pl.ds(2, rows), pl.ds(SUB + cols, SUB)] = side


def share(pad, number, rows, cols, da, dc, o):
    row = number(AT_ROW, o).astype(jnp.int32) - 1 + da * rows
    col = number(AT_COL, o).astype(jnp.int32) - 1 + dc * cols
    row = jnp.clip(row, -2, rows) + 2
    col = jnp.clip(col, -2, cols) + SUB
    terms = [number(k, o) * pad[row + k // 2, pl.ds(col + k % 2, 1), :] for k in range(4)]
    return (terms[0] + terms[1]) + (terms[2] + terms[3])


def own_shift(number):
    sub = lax.broadcasted_iota(jnp.int32, (SUB, LANES), 0)
    shift = jnp.zeros((SUB, LANES), F32)
    for o in range(SUB):
        shift = jnp.where(sub == o, number(AT_OBS, o), shift)
    return shift


def pad_kernel(cells, pad, sem):
    rows, cols = (cells.shape[0], cells.shape[1])
    copy = pltpu.make_async_copy(cells, pad.at[pl.ds(2, rows), pl.ds(SUB, cols)], sem)
    copy.start()
    clear_rim(pad, rows, cols)
    copy.wait()


def fetch_params(batch, mine, ends_0, ends_1, params, sems):
    copies = []
    for n, source in enumerate((ends_0, mine, ends_1)):
        copies.append(pltpu.make_async_copy(source.at[batch], params.at[n], sems.at[n]))
        copies[-1].start()
    for copy in copies:
        copy.wait()
    even = is_even("lat")
    above, below = (jnp.where(even, 2, 0), jnp.where(even, 0, 2))
    return [lambda kind, o, spot=spot: params[spot, kind, o] for spot in (above, 1, below)]


def hold_sides(sides_0, sides_1, sides):
    rows = sides_0.shape[0] - SUB
    even = is_even("lon")
    first, second = (sides_0[pl.ds(0, rows), :], sides_1[pl.ds(0, rows), :])
    sides[...] = jnp.zeros_like(sides)
    sides[0, pl.ds(SUB, rows), :] = jnp.where(even, second, first)
    sides[1, pl.ds(SUB, rows), :] = jnp.where(even, first, second)


def side_share(sides, side, number, rows, cols, da, o):
    row = number(AT_ROW, o).astype(jnp.int32) - 1 + da * rows
    row = jnp.clip(row, -2, rows) + SUB
    used = number(AT_COL, o).astype(jnp.int32) == (0, cols)[side]
    terms = [jnp.where(used, number(side + 2 * k, o), 0.0) * sides[side, pl.ds(row + k, 1), :] for k in range(2)]
    return terms[0] + terms[1]


def send_shares(shares, out_ref):
    means = [jnp.mean(part, axis=-1, keepdims=True) for part in shares]
    lane = lax.broadcasted_iota(jnp.int32, (SUB, LANES), 1)
    packed = jnp.where(lane < MEAN_LANES, means[0], jnp.where(lane < 2 * MEAN_LANES, means[1], means[2]))
    rows = [part - mean for part, mean in zip(shares, means)]
    slot = jnp.concatenate(rows + [packed], axis=0).astype(BF16)
    out_ref[...] = jnp.broadcast_to(slot, out_ref.shape)


def column_kernel(mine, sides_0, sides_1, ends_0, ends_1, pad, out_ref, block, sides, params, sems):
    rows, cols = (pad.shape[0] - 4, pad.shape[1] - 2 * SUB)
    hold_sides(sides_0, sides_1, sides)
    numbers = fetch_params(0, mine, ends_0, ends_1, params, sems)
    for n, da in enumerate(NEAR):
        for o in range(SUB):
            total = share(pad, numbers[n], rows, cols, da, 0, o)
            for side in range(2):
                total = total + side_share(sides, side, numbers[n], rows, cols, da, o)
            block[n, pl.ds(o, 1), :] = total
    send_shares([block[0], block[1] - own_shift(numbers[1]), block[2]], out_ref)


def later_kernel(mine, sides_0, sides_1, ends_0, ends_1, pad, out_ref, sides, params, sems):
    rows, cols = (pad.shape[0] - 4, pad.shape[1] - 2 * SUB)
    hold_sides(sides_0, sides_1, sides)
    numbers = fetch_params(1, mine, ends_0, ends_1, params, sems)
    for n, da in enumerate(NEAR):
        for o in range(SUB):
            at = pl.ds(n * SUB + o, 1)
            out_ref[0, at, :] = side_share(sides, 0, numbers[n], rows, cols, da, o)
            out_ref[1, at, :] = share(pad, numbers[n], rows, cols, da, 0, o)
            out_ref[2, at, :] = side_share(sides, 1, numbers[n], rows, cols, da, o)
    out_ref[len(NEAR), pl.ds(0, SUB), :] = own_shift(numbers[1])


def window_start(lat_count, my_lat):
    return 0 if lat_count <= WIN else jnp.clip(my_lat - REACH, 0, lat_count - WIN)


def row_of(block, j):
    return jnp.broadcast_to(block[j:j + 1, :], (SUB, LANES))


def reciprocal(value):
    guess = pl.reciprocal(value, approx=True)
    return guess * (2.0 - value * guess)


def eliminate(systems):
    systems = [list(blocks) for blocks in systems]
    inverses = [[] for _ in systems]
    for k in range(len(systems[0]) - 1):
        for blocks, inverse in zip(systems, inverses):
            inverse.append(eliminate_block(blocks, k))
    return [(inverse, blocks[-1][:1]) for inverse, blocks in zip(inverses, systems)]


def eliminate_block(blocks, k):
    count = len(blocks) - 1
    sub = lax.broadcasted_iota(jnp.int32, (SUB, LANES), 0)
    lane = lax.broadcasted_iota(jnp.int32, (SUB, LANES), 1)
    here = (lane >= k * SUB) & (lane < (k + 1) * SUB)
    column = [
        [jnp.broadcast_to(blocks[i][:, k * SUB + j:k * SUB + j + 1], (SUB, LANES)) for j in range(SUB)]
        for i in range(k, count + 1)
    ]
    diag = list(column[0])
    full = jnp.where(here, jnp.where(lane - k * SUB == sub, 1.0, 0.0), blocks[k])
    lower = full
    scale = jnp.zeros((SUB, LANES), F32)
    for j in range(0, SUB, 2):
        a, b, c = (row_of(diag[j], j), row_of(diag[j + 1], j), row_of(diag[j + 1], j + 1))
        det = a * c - b * b
        over_det = reciprocal(det)
        first = jnp.where(sub == j, -c, jnp.where(sub == j + 1, b, diag[j] * c - diag[j + 1] * b))
        second = jnp.where(sub == j, b, jnp.where(sub == j + 1, -a, diag[j + 1] * a - diag[j] * b))
        first, second = (first * over_det, second * over_det)
        other = (sub != j) & (sub != j + 1)
        for n in range(j + 2, SUB):
            diag[n] = jnp.where(other, diag[n], 0.0) - first * row_of(diag[n], j) - second * row_of(diag[n], j + 1)
        full = jnp.where(other, full, 0.0) - first * row_of(full, j) - second * row_of(full, j + 1)
        over_a = reciprocal(a)
        top, bottom = (row_of(lower, j), row_of(lower, j + 1))
        below = sub > j + 1
        lower = lower - jnp.where(sub == j + 1, b * over_a, jnp.where(below, first, 0.0)) * top
        lower = lower - jnp.where(below, second, 0.0) * bottom
        scale = jnp.where(sub == j, lax.rsqrt(a), jnp.where(sub == j + 1, lax.rsqrt(det * over_a), scale))
    pivot = [row_of(full, j) for j in range(SUB)]
    for i in range(k + 1, count + 1):
        terms = [column[i - k][j] * pivot[j] for j in range(SUB)]
        while len(terms) > 1:
            terms = [terms[n] + terms[n + 1] for n in range(0, len(terms), 2)]
        blocks[i] = jnp.where(here, 0.0, blocks[i]) - terms[0]
    return jnp.where(lane < (k + 1) * SUB, lower * scale, 0.0)


def tile_block(near_ref, lat, lon, lat_count, lon_count):
    lane = lax.broadcasted_iota(jnp.int32, (SUB, LANES), 1)
    scaled, means = (jnp.zeros((SUB, LANES), F32), jnp.zeros((SUB, LANES), F32))
    for n, da in enumerate(NEAR):
        source = lat - da
        inside = True
        if isinstance(source, int):
            if not 0 <= source < lat_count:
                continue
        else:
            inside = (source >= 0) & (source < lat_count)
            source = jnp.clip(source, 0, lat_count - 1)
        slot = near_ref[source * lon_count + lon].astype(F32)
        values, mean = (slot[n * SUB:(n + 1) * SUB], slot[len(NEAR) * SUB:])
        if inside is not True:
            values, mean = (jnp.where(inside, values, 0.0), jnp.where(inside, mean, 0.0))
        scaled = scaled + values
        lanes = (lane >= n * MEAN_LANES) & (lane < (n + 1) * MEAN_LANES)
        means = jnp.where(lanes, mean, means)
    return scaled, jnp.sum(means, axis=-1, keepdims=True) * (-1.0 / MEAN_LANES)


def batch_maps(lat_count, lon_count, near_ref, marks):
    held = min(WIN, lat_count)
    my_lat = lax.axis_index("lat")
    start = window_start(lat_count, my_lat)
    scaled, innov, picked = ([], [], [[] for _ in marks])
    for j in range(held):
        offset = start + j - my_lat + REACH
        inside = (offset >= 0) & (offset < WIN)
        offset = jnp.clip(offset, 0, WIN - 1)
        for e in range(lon_count):
            values, value = tile_block(near_ref, start + j, e, lat_count, lon_count)
            scaled.append(values)
            innov.append(value)
            for pick, mark in zip(picked, marks):
                pick.append(jnp.full((SUB, LANES), jnp.where(inside, mark(offset, e), 0.0)))
    scaled = jnp.concatenate(scaled, axis=0).astype(BF16)
    innov = jnp.concatenate(innov, axis=0).astype(BF16).astype(F32)
    rounded = scaled.astype(F32)
    weighted = [rounded * jnp.concatenate(pick, axis=0) for pick in picked]
    grams = lax.dot_general(
        jnp.concatenate(weighted, axis=1).astype(BF16),
        scaled,
        (((0,), (0,)), ((), ())),
        preferred_element_type=F32,
    )
    sub = lax.broadcasted_iota(jnp.int32, (SUB, LANES), 0)
    lane = lax.broadcasted_iota(jnp.int32, (SUB, LANES), 1)
    members = LANES
    systems = []
    for n, part in enumerate(weighted):
        blocks = []
        for k in range(members // SUB):
            at = n * members + k * SUB
            blocks.append(grams[at:at + SUB, :] + jnp.where(lane - k * SUB == sub, members - 1.0, 0.0))
        proj = jnp.sum((part * innov).reshape(-1, SUB, LANES), axis=0)
        blocks.append(jnp.broadcast_to(jnp.sum(proj, axis=0, keepdims=True), (SUB, LANES)))
        systems.append(blocks)
    maps = []
    for inverse, weights in eliminate(systems):
        flipped = jnp.concatenate(inverse, axis=0) * (members - 1.0) ** 0.5 - weights
        maps.append(flipped - jnp.mean(flipped, axis=-1, keepdims=True) + 1.0 / members)
    return maps


def exact_dot(a, b, contract_b):
    return lax.dot_general(
        a, b, (((1,), (contract_b,)), ((), ())), precision=lax.Precision.HIGHEST, preferred_element_type=F32
    )


def first_kernel(lat_count, lon_count, near_ref, marks_ref, sides_0, sides_1, later, out_ref, map_ref, marks, sems):
    rows = sides_0.shape[0] - SUB
    side = pl.ds(rows, SUB)
    copies = []
    for n, source in enumerate((sides_0.at[side], marks_ref.at[0], sides_1.at[side])):
        copies.append(pltpu.make_async_copy(source, marks.at[n], sems.at[n]))
        copies[-1].start()
    for copy in copies:
        copy.wait()
    even = is_even("lon")
    left, right = (jnp.where(even, 2, 0), jnp.where(even, 0, 2))
    picks = [lambda offset, e, spot=spot: marks[spot, offset, e] for spot in (left, 1, right)]
    maps = batch_maps(lat_count, lon_count, near_ref, picks)
    map_ref[...] = maps[1]
    moved = [exact_dot(later[n], flipped, 1) for n, flipped in enumerate(maps)]
    moved = moved[0] + moved[1] + moved[2]
    shares = [moved[n * SUB:(n + 1) * SUB] for n in range(len(NEAR))]
    shares[1] = shares[1] - later[len(NEAR), pl.ds(0, SUB), :]
    send_shares(shares, out_ref)


def last_kernel(lat_count, lon_count, near_ref, marks_ref, map_ref, pad, out_ref, result, marks, mark_sem, out_sem):
    parts = out_sem.shape[0]
    rows, cols = (pad.shape[0] - 4, pad.shape[1] - 2 * SUB)
    copy = pltpu.make_async_copy(marks_ref.at[1], marks, mark_sem)
    copy.start()
    copy.wait()
    maps = batch_maps(lat_count, lon_count, near_ref, [lambda offset, e: marks[offset, e]])
    flipped = exact_dot(maps[0], map_ref[...], 0)
    high = flipped.astype(BF16)
    low = (flipped - high.astype(F32)).astype(BF16)
    right = jnp.concatenate(
        [jnp.concatenate([high, high], axis=1), jnp.concatenate([low, jnp.zeros_like(low)], axis=1)], axis=0
    )
    copies = []
    size = rows // parts
    for n in range(parts):
        part = pl.ds(n * size * cols, size * cols)
        value = pad[pl.ds(2 + n * size, size), pl.ds(SUB, cols), :].reshape(size * cols, LANES)
        upper = value.astype(BF16)
        rest = (value - upper.astype(F32)).astype(BF16)
        both = lax.dot_general(
            jnp.concatenate([upper, rest], axis=1), right, (((1,), (1,)), ((), ())), preferred_element_type=F32
        )
        result[part, :] = both[:, :LANES] + both[:, LANES:]
        copies.append(pltpu.make_async_copy(result.at[part], out_ref.at[part], out_sem.at[n]))
        copies[-1].start()
    for out_copy in copies:
        out_copy.wait()


def local(ensemble, observed, precision, interp_weight, stencil, owned, pattern):
    rows, cols, members = ensemble.shape
    batches = observed.shape[0]
    lat_count, lon_count = (lax.axis_size("lat"), lax.axis_size("lon"))
    tiles = lat_count * lon_count
    column = len(NEAR) * SUB
    slots = (tiles, column + SUB, members)
    vmem = pl.BlockSpec(memory_space=pltpu.VMEM)
    anywhere = pl.BlockSpec(memory_space=pl.ANY)
    hbm = pl.BlockSpec(memory_space=pltpu.HBM)
    megabyte = 1024 * 1024

    def shape(*dims, dtype=F32):
        return jax.ShapeDtypeStruct(dims, dtype)

    def call(kernel, name, specs, out_shape, scratch, *operands, out_specs=None, limit=48):
        return pl.pallas_call(
            kernel,
            out_shape=out_shape,
            in_specs=specs,
            out_specs=out_specs or jax.tree.map(lambda _: vmem, out_shape),
            scratch_shapes=scratch,
            compiler_params=pltpu.CompilerParams(vmem_limit_bytes=limit * megabyte),
            name=name,
        )(*operands)

    def trade(blocks, axis):
        count, wraps = ((lon_count, True) if axis == "lon" else (lat_count, False))
        second = swap(blocks[1], axis, 1, count, wraps)
        first = swap(blocks[0], axis, 0, count, wraps)
        return (first, second)

    def exchange(blocks):
        return lax.all_to_all(blocks, ("lat", "lon"), split_axis=0, concat_axis=0, tiled=True)

    by_row = pattern.reshape(batches, WIN, 1, lon_count)
    small = (observed, precision, interp_weight, stencil, owned, by_row)
    side = shape(rows + SUB, members)
    block = shape(batches, SUB, LANES)
    mine, marks, *sides = call(
        functools.partial(start_kernel, cols + 2),
        "start",
        [hbm] * 7,
        (block, block, side, side),
        [pltpu.VMEM(array.shape, array.dtype) for array in small]
        + [pltpu.VMEM((rows, SUB, members), F32)] * 2
        + [pltpu.SemaphoreType.DMA((8,))],
        *small,
        ensemble,
        limit=63,
    )
    sides = trade(sides, "lon")
    ends = trade((mine, mine), "lat")
    padded = shape(rows + 4, cols + 2 * SUB, members)
    pad = call(pad_kernel, "pad", [hbm], padded, [pltpu.SemaphoreType.DMA], ensemble)
    near_tiles = (mine, *sides, *ends, pad)
    held_sides = pltpu.VMEM((2, rows + 2 * SUB, members), F32)
    numbers = [pltpu.SMEM((3, SUB, LANES), F32), pltpu.SemaphoreType.DMA((3,))]
    shares = call(
        column_kernel,
        "column_shares",
        [vmem] * 6,
        shape(*slots, dtype=BF16),
        [pltpu.VMEM((3, SUB, members), F32), held_sides] + numbers,
        *near_tiles,
    )
    near = exchange(shares)
    later = call(
        later_kernel, "later_shares", [vmem] * 6, shape(4, column, members), [held_sides] + numbers, *near_tiles
    )
    shares, first_map = call(
        functools.partial(first_kernel, lat_count, lon_count),
        "first_batch",
        [vmem] * 5,
        (shape(*slots, dtype=BF16), shape(members, members)),
        numbers,
        near,
        marks,
        *sides,
        later,
    )
    near = exchange(shares)
    parts = 8
    result = call(
        functools.partial(last_kernel, lat_count, lon_count),
        "second_batch",
        [vmem] * 4,
        shape(rows * cols, members),
        [
            pltpu.VMEM((rows * cols, members), F32),
            pltpu.SMEM((SUB, LANES), F32),
            pltpu.SemaphoreType.DMA,
            pltpu.SemaphoreType.DMA((parts,)),
        ],
        near,
        marks,
        first_map,
        pad,
        out_specs=anywhere,
    )
    return result.reshape(rows, cols, members)


def solution(mesh):
    placed = (
        P("lat", "lon", None),
        P(None, "lat", "lon", None),
        P(None, "lat", "lon", None),
        P(None, "lat", "lon", None, None),
        P(None, "lat", "lon", None, None),
        P(None, "lat", "lon", None),
        P(None, "lat", "lon", None, None),
    )
    return jax.shard_map(
        local, mesh=mesh, in_specs=placed, out_specs=P("lat", "lon", None), check_vma=False
    )
```

time: 67.8 us -> 60.9 us (0.90)
  starting transfers between devices: 19.1 us -> 11.8 us
  Pallas kernels: 18.7 us -> 23.1 us
  waiting for transfers between devices: 13.3 us -> 9.42 us
    ppermute x10 -> x4, waiting for transfers between devices: 6.67 us -> 0.03 us  [swap(): return lax.ppermute(block, axis, route)]
    ppermute x10 -> x4, starting transfers between devices: 13.6 us -> 9.19 us  [swap(): return lax.ppermute(block, axis, route)]
    pallas_call x9 -> x6, Pallas kernels: 18.7 us -> 23.1 us  [call(): pl.pallas_call(kernel, out_shape=out_shape, in_specs=specs, out_specs=out...]
    all_to_all x1, starting transfers between devices: 5.45 us -> 2.6 us  [exchange(): lax.all_to_all(blocks, ('lat', 'lon'), split_axis=0, concat_axis=0, tiled...]
    all_to_all x1, waiting for transfers between devices: 6.61 us -> 9.38 us  [exchange(): lax.all_to_all(blocks, ('lat', 'lon'), split_axis=0, concat_axis=0, tiled...]
    squeeze x1 -> x0, local copies, waits for them, and re-layouts: 0.74 us -> none  [local(): ends = trade((mine[0], mine[0]), 'lat')]
    unnamed x9 -> x7, local copies, waits for them, and re-layouts: 3.19 us -> 2.73 us
  transfers between devices with their start and end apart: 11 -> 5, of which waited for: 5 -> 1; matrix products, arithmetic and copies ran while one was open for 1% -> 0% of each run, Pallas kernels for 3% -> 2%
where the time goes in v2:
time: 60.9 us; the launch traced here: 60.6 us
  Pallas kernels  23.1 us (38%)
  blocking collectives  12.7 us (21%)
  starting transfers between devices  11.8 us (19%)
  waiting for transfers between devices  9.42 us (15%)
  local copies, waits for them, and re-layouts  3.33 us (5%)
    pallas_call x6, Pallas kernels, call(): pl.pallas_call(kernel, out_shape=out_shape, in_specs=specs, out_specs=out...  23.1 us
    all_to_all x1, blocking collectives, exchange(): lax.all_to_all(blocks, ('lat', 'lon'), split_axis=0, concat_axis=0, tiled...  12.7 us
    all_to_all x1, waiting for transfers between devices, exchange(): lax.all_to_all(blocks, ('lat', 'lon'), split_axis=0, concat_axis=0, tiled...  9.38 us
    ppermute x4, starting transfers between devices, swap(): return lax.ppermute(block, axis, route)  9.19 us
    unnamed x7, local copies, waits for them, and re-layouts  2.73 us
    all_to_all x1, starting transfers between devices, exchange(): lax.all_to_all(blocks, ('lat', 'lon'), split_axis=0, concat_axis=0, tiled...  2.6 us
  transfers between devices with their start and end apart: 5, of which 1 were waited for; matrix products, arithmetic and copies ran while one was open for 0% of the time, Pallas kernels for 2%

profile of v2, /device:TPU:0, one launch (start us, length us, event | category | flops | bytes accessed | tf_op | source)
XLA Modules:
  0.0 60.6 jit_solution(17736075511085488572)
XLA Ops:
  0.0 0.7 %copy.11 = s32[2,1,1,5,8]{4,0,3,2,1:T(2,128)S(1)} copy(s32[2,1,1,5,8]{4,2,3,1,0:T(1,128)} %param.13) | data formatting | bytes 640 | tf_op args[6]
  0.7 0.6 copy.9.pattern
  1.3 1.8 %start.1 = (f32[2,8,128]{2,1,0:T(8,128)}, f32[2,8,128]{2,1,0:T(8,128)}, f32[40,128]{1,0:T(8,128)}, f32[40,128]{1,0:T(8,128)}) custom-call(f32[2,1,1,8]{3,2,1,0:T(1,128)} %observed.1, f32[2,1,1,8]{3,2,1,0:T(1,128)} %precision.1, f32[2,1,1,4,8]{4,3,2,1,0:T(4,128)} %weight.1, s32[2,1,1,4,8]{4,3,2,1,0:T(4,128)} %stencil.1, s32[2,1,1,8]{3,2,1,0:T(1,128)} %owned.1, ...), custom_call_target="tpu_custom_call" | custom-call | tf_op jit(solution)/shard_map/start/pallas_call | solution.py:371
  3.1 0.5 collective-permute-start
  3.6 3.6 %collective-permute-start.1 = (f32[40,128]{1,0:T(8,128)}, f32[40,128]{1,0:T(8,128)S(1)}, u32[]{:S(2)}, u32[]{:S(2)}) collective-permute-start(f32[40,128]{1,0:T(8,128)} %get-tuple-element.13), channel_id=1, source_target_pairs={{0,7},{1,2},{2,1},{3,4},{4,3},{5,6},{6,5},{7,0},{8,15},{9,10},{10,... | collective-permute-start | bytes 61448 | tf_op jit(solution)/shard_map/ppermute | solution.py:26
  7.2 0.6 %collective-permute-start.3 = (f32[2,8,128]{2,1,0:T(8,128)}, f32[2,8,128]{2,1,0:T(8,128)S(1)}, u32[]{:S(2)}, u32[]{:S(2)}) collective-permute-start(f32[2,8,128]{2,1,0:T(8,128)} %get-tuple-element.11.mine), channel_id=1, source_target_pairs={{8,16},{16,8},{9,17},{17,9},{10,18},{18,10},{11,19},{19,11},{12,20... | collective-permute-start | bytes 24584 | tf_op jit(solution)/shard_map/ppermute | solution.py:26
  7.8 4.5 %collective-permute-start.2 = (f32[2,8,128]{2,1,0:T(8,128)}, f32[2,8,128]{2,1,0:T(8,128)S(1)}, u32[]{:S(2)}, u32[]{:S(2)}) collective-permute-start(f32[2,8,128]{2,1,0:T(8,128)} %get-tuple-element.11.mine), channel_id=1, source_target_pairs={{0,8},{8,0},{16,24},{24,16},{1,9},{9,1},{17,25},{25,17},{2,10},{10... | collective-permute-start | bytes 24584 | tf_op jit(solution)/shard_map/ppermute | solution.py:26
  12.3 0.0 copy-start
  12.3 1.6 %copy-done = f32[32,128,128]{2,1,0:T(8,128)S(1)} copy-done((f32[32,128,128]{2,1,0:T(8,128)S(1)}, f32[32,128,128]{2,1,0:T(8,128)}, u32[]{:S(2)}) %copy-start) | copy-done | bytes 2097176
  13.9 0.0 copy-start.1
  13.9 0.2 pad.1
  14.1 0.0 collective-permute-done.3.ends_1
  14.1 0.0 collective-permute-done.2.ends_0
  14.1 0.0 collective-permute-done.sides_0
  14.1 0.0 collective-permute-done.1.sides_1
  14.1 0.4 copy-done.1
  14.6 1.8 %column_shares.1 = bf16[32,32,128]{2,1,0:T(8,128)(2,1)} custom-call(f32[2,8,128]{2,1,0:T(8,128)S(1)} %copy-done.1, f32[40,128]{1,0:T(8,128)S(1)} %collective-permute-done.sides_0, f32[40,128]{1,0:T(8,128)S(1)} %collective-permute-done.1.sides_1, f32[2,8,128]{2,1,0:T(8,128)S(1)} %collective-permute-done.2.ends_0, ...), custom_call_target="tpu_custom_call" | custom-call | tf_op jit(solution)/shard_map/column_shares/pallas_call | solution.py:371
  16.4 0.0 copy-start.2
  16.4 2.6 %all-to-all-start = ((bf16[32,32,128]{2,1,0:T(8,128)(2,1)}), bf16[32,32,128]{2,1,0:T(8,128)(2,1)S(1)}, u32[]{:S(2)}, u32[]{:S(2)}) async-start(bf16[32,32,128]{2,1,0:T(8,128)(2,1)} %column_shares.1), calls=%async_computation | async-start | bytes 524288 | tf_op jit(solution)/shard_map/all_to_all | solution.py:388
  19.0 1.2 %later_shares.1.later = f32[4,24,128]{2,1,0:T(8,128)S(1)} custom-call(f32[2,8,128]{2,1,0:T(8,128)S(1)} %copy-done.1, f32[40,128]{1,0:T(8,128)S(1)} %collective-permute-done.sides_0, f32[40,128]{1,0:T(8,128)S(1)} %collective-permute-done.1.sides_1, f32[2,8,128]{2,1,0:T(8,128)S(1)} %collective-permute-done.2.ends_0, ...), custom_call_target="tpu_custom_call" | custom-call | tf_op jit(solution)/shard_map/later_shares/pallas_call | solution.py:371
  20.3 9.4 %all-to-all-done.near_ref = bf16[32,32,128]{2,1,0:T(8,128)(2,1)S(1)} async-done(((bf16[32,32,128]{2,1,0:T(8,128)(2,1)}), bf16[32,32,128]{2,1,0:T(8,128)(2,1)S(1)}, u32[]{:S(2)}, u32[]{:S(2)}) %all-to-all-start) | async-done | bytes 262176 | tf_op jit(solution)/shard_map/all_to_all | solution.py:388
  29.6 0.0 copy-done.2
  29.6 10.1 %first_batch.1 = (bf16[32,32,128]{2,1,0:T(8,128)(2,1)S(1)}, f32[128,128]{1,0:T(8,128)S(1)}) custom-call(bf16[32,32,128]{2,1,0:T(8,128)(2,1)S(1)} %all-to-all-done.near_ref, f32[2,8,128]{2,1,0:T(8,128)S(1)} %copy-done.2, f32[40,128]{1,0:T(8,128)S(1)} %collective-permute-done.sides_0, f32[40,128]{1,0:T(8,128)S(1)} %collective-permute-done.1.sides_1, ...), custom_call_target="tpu_custom_call" | custom-call | tf_op jit(solution)/shard_map/first_batch/pallas_call | solution.py:371
  39.8 12.7 %all_to_all.10.near_ref = bf16[32,32,128]{2,1,0:T(8,128)(2,1)S(1)} all-to-all(bf16[32,32,128]{2,1,0:T(8,128)(2,1)S(1)} %get-tuple-element.15), channel_id=1, replica_groups=mesh['lat'=4,'lon'=8] {'lat','lon'}, dimensions={0} | all-to-all | bytes 524288 | tf_op jit(solution)/shard_map/all_to_all | solution.py:388
  52.5 7.9 %second_batch.1 = f32[4096,128]{1,0:T(8,128)} custom-call(bf16[32,32,128]{2,1,0:T(8,128)(2,1)S(1)} %all_to_all.10.near_ref, f32[2,8,128]{2,1,0:T(8,128)S(1)} %copy-done.2, f32[128,128]{1,0:T(8,128)S(1)} %get-tuple-element.16.map_ref, f32[36,144,128]{2,1,0:T(8,128)S(1)} %pad.1), custom_call_target="tpu_custom_call" | custom-call | tf_op jit(solution)/shard_map/second_batch/pallas_call | solution.py:371
Async XLA Ops:
  3.1 11.0 %collective-permute-start = (f32[40,128]{1,0:T(8,128)}, f32[40,128]{1,0:T(8,128)S(1)}, u32[]{:S(2)}, u32[]{:S(2)}) collective-permute-start(f32[40,128]{1,0:T(8,128)} %get-tuple-element.12), channel_id=1, source_target_pairs={{0,1},{1,0},{2,3},{3,2},{4,5},{5,4},{6,7},{7,6},{8,9},{9,8},{10,11... | collective-permute-start | bytes 61448 | tf_op jit(solution)/shard_map/ppermute | solution.py:26
  3.6 10.5 %collective-permute-start.1 = (f32[40,128]{1,0:T(8,128)}, f32[40,128]{1,0:T(8,128)S(1)}, u32[]{:S(2)}, u32[]{:S(2)}) collective-permute-start(f32[40,128]{1,0:T(8,128)} %get-tuple-element.13), channel_id=1, source_target_pairs={{0,7},{1,2},{2,1},{3,4},{4,3},{5,6},{6,5},{7,0},{8,15},{9,10},{10,... | collective-permute-start | bytes 61448 | tf_op jit(solution)/shard_map/ppermute | solution.py:26
  7.2 6.9 %collective-permute-start.3 = (f32[2,8,128]{2,1,0:T(8,128)}, f32[2,8,128]{2,1,0:T(8,128)S(1)}, u32[]{:S(2)}, u32[]{:S(2)}) collective-permute-start(f32[2,8,128]{2,1,0:T(8,128)} %get-tuple-element.11.mine), channel_id=1, source_target_pairs={{8,16},{16,8},{9,17},{17,9},{10,18},{18,10},{11,19},{19,11},{12,20... | collective-permute-start | bytes 24584 | tf_op jit(solution)/shard_map/ppermute | solution.py:26
  7.8 6.3 %collective-permute-start.2 = (f32[2,8,128]{2,1,0:T(8,128)}, f32[2,8,128]{2,1,0:T(8,128)S(1)}, u32[]{:S(2)}, u32[]{:S(2)}) collective-permute-start(f32[2,8,128]{2,1,0:T(8,128)} %get-tuple-element.11.mine), channel_id=1, source_target_pairs={{0,8},{8,0},{16,24},{24,16},{1,9},{9,1},{17,25},{25,17},{2,10},{10... | collective-permute-start | bytes 24584 | tf_op jit(solution)/shard_map/ppermute | solution.py:26
  12.3 1.6 %copy-start = (f32[32,128,128]{2,1,0:T(8,128)S(1)}, f32[32,128,128]{2,1,0:T(8,128)}, u32[]{:S(2)}) copy-start(f32[32,128,128]{2,1,0:T(8,128)} %cells.3) | copy-start | bytes 6291460
  13.9 0.7 %copy-start.1 = (f32[2,8,128]{2,1,0:T(8,128)S(1)}, f32[2,8,128]{2,1,0:T(8,128)}, u32[]{:S(2)}) copy-start(f32[2,8,128]{2,1,0:T(8,128)} %get-tuple-element.11.mine) | copy-start | bytes 24580
  16.4 13.2 %copy-start.2 = (f32[2,8,128]{2,1,0:T(8,128)S(1)}, f32[2,8,128]{2,1,0:T(8,128)}, u32[]{:S(2)}) copy-start(f32[2,8,128]{2,1,0:T(8,128)} %get-tuple-element.14.marks_ref) | copy-start | bytes 24580
  16.4 13.2 %all-to-all-start = ((bf16[32,32,128]{2,1,0:T(8,128)(2,1)}), bf16[32,32,128]{2,1,0:T(8,128)(2,1)S(1)}, u32[]{:S(2)}, u32[]{:S(2)}) async-start(bf16[32,32,128]{2,1,0:T(8,128)(2,1)} %column_shares.1), calls=%async_computation | async-start | bytes 524288 | tf_op jit(solution)/shard_map/all_to_all | solution.py:388

commit v3 on v1

--- a/solution.py
+++ b/solution.py
@@ -11,37 +11,59 @@
 SUB = 8
 LANES = 128
 NEAR = (-1, 0, 1)
+AROUND = tuple((dc, da) for dc in NEAR for da in NEAR)
+TRADES = ((0, None), (1, None), (None, 0), (None, 1), (0, 0), (0, 1), (1, 0), (1, 1))
 AT_ROW, AT_COL, AT_OBS = (4, 5, 6)
 F32 = jnp.float32
 BF16 = jnp.bfloat16
 
 
-def swap(block, axis, kind, count, wraps):
-    route = []
-    for place in range(count):
-        partner = place + (1 if place % 2 == kind else -1)
-        if wraps or 0 <= partner < count:
-            route.append((place, partner % count))
-    return lax.ppermute(block, axis, route)
+def partner(place, kind):
+    return place if kind is None else place + (1 if place % 2 == kind else -1)
+
+
+def trade(blocks, lat_count, lon_count):
+    results = []
+    for (lat_kind, lon_kind), block in zip(TRADES, blocks):
+        route = []
+        for lat in range(lat_count):
+            for lon in range(lon_count):
+                other = partner(lat, lat_kind)
+                if 0 <= other < lat_count:
+                    target = other * lon_count + partner(lon, lon_kind) % lon_count
+                    route.append((lat * lon_count + lon, target))
+        results.append(lax.ppermute(block, ("lat", "lon"), route))
+    return results
 
 
 def is_even(axis):
     return lax.rem(lax.axis_index(axis), 2) == 0
 
 
-def start_kernel(
-    width, observed, precision, weight, stencil, owned, cells, params_ref, sides_0, sides_1,
-    observed_v, precision_v, weight_v, stencil_v, owned_v, left_v, right_v, sems
-):
-    batches, cols = (observed.shape[0], cells.shape[1])
+def toward(axis, kind):
+    if kind is None:
+        return 0
+    return jnp.where(is_even(axis), 1 - 2 * kind, 2 * kind - 1)
+
+
+def kind_at(axis, step):
+    return jnp.where(is_even(axis), (1 - step) // 2, (1 + step) // 2)
+
+
+def start_kernel(width, observed, precision, weight, stencil, owned, cells, params_ref, *refs):
+    outs, (observed_v, precision_v, weight_v, stencil_v, owned_v, cols_v, rows_v, sems) = (refs[:8], refs[8:])
+    batches = observed.shape[0]
+    rows, cols = (cells.shape[0], cells.shape[1])
     pairs = (
         (observed, observed_v),
         (precision, precision_v),
         (weight, weight_v),
         (stencil, stencil_v),
         (owned, owned_v),
-        (cells.at[:, pl.ds(0, SUB)], left_v),
-        (cells.at[:, pl.ds(cols - SUB, SUB)], right_v),
+        (cells.at[:, pl.ds(0, SUB)], cols_v.at[0]),
+        (cells.at[:, pl.ds(cols - SUB, SUB)], cols_v.at[1]),
+        (cells.at[0], rows_v.at[0]),
+        (cells.at[rows - 1], rows_v.at[1]),
     )
     copies = [pltpu.make_async_copy(source, target, sems.at[n]) for n, (source, target) in enumerate(pairs)]
     for copy in copies:
@@ -57,13 +79,23 @@
         params_ref[b, pl.ds(AT_ROW, 1), pl.ds(0, SUB)] = row
         params_ref[b, pl.ds(AT_COL, 1), pl.ds(0, SUB)] = corner - row * width
         params_ref[b, pl.ds(AT_OBS, 1), pl.ds(0, SUB)] = observed_v[b, 0] * root
-    rows = cells.shape[0]
-    even = is_even("lon")
-    left, right = (left_v[:, 0, :], right_v[:, SUB - 1, :])
-    sides_0[pl.ds(0, rows), :] = jnp.where(even, right, left)
-    sides_1[pl.ds(0, rows), :] = jnp.where(even, left, right)
-    sides_0[pl.ds(rows, SUB), :] = params_ref[1]
-    sides_1[pl.ds(rows, SUB), :] = params_ref[1]
+    lon_even, lat_even = (is_even("lon"), is_even("lat"))
+    column = (cols_v[0, :, 0, :], cols_v[1, :, SUB - 1, :])
+    edge = (rows_v[0], rows_v[1])
+    sides = [jnp.where(lon_even, column[1 - kind], column[kind]) for kind in range(2)]
+    ends = [jnp.where(lat_even, edge[1 - kind], edge[kind]) for kind in range(2)]
+    for (lat_kind, lon_kind), out in zip(TRADES, outs):
+        if lat_kind is None:
+            block = sides[lon_kind]
+        elif lon_kind is None:
+            block = ends[lat_kind]
+        else:
+            last = jnp.where(lon_even, 1 - lon_kind, lon_kind) == 1
+            block = jnp.where(last, ends[lat_kind][cols - 1:], ends[lat_kind][:1])
+            block = jnp.broadcast_to(block, (SUB, LANES))
+        size = block.shape[0]
+        out[pl.ds(0, size), :] = block
+        out[pl.ds(size, SUB), :] = params_ref[1]
 
 
 def clear_rim(pad, rows, cols):
@@ -100,75 +132,82 @@
     copy.wait()
 
 
-def column_kernel(mine, sides_0, sides_1, ends_0, ends_1, pad, own_ref, out_0, out_1, block, sides, params, sems):
-    rows, cols = (pad.shape[0] - 4, pad.shape[1] - 2 * SUB)
-    lon_even, lat_even = (is_even("lon"), is_even("lat"))
-    copies = []
-    for n, source in enumerate((ends_0, mine.at[0], ends_1)):
-        copies.append(pltpu.make_async_copy(source, params.at[n], sems.at[n]))
-        copies[-1].start()
-    sides[...] = jnp.zeros_like(sides)
-    left = jnp.where(lon_even, sides_1[...], sides_0[...])
-    right = jnp.where(lon_even, sides_0[...], sides_1[...])
-    sides[0, pl.ds(SUB, rows), :] = left[:rows]
-    sides[1, pl.ds(SUB, rows), :] = right[:rows]
-    lane = lax.broadcasted_iota(jnp.int32, (SUB, LANES), 1)
-    packed = jnp.where(lane < SUB, left[rows:], pltpu.roll(mine[1], SUB, 1))
-    packed = jnp.where(lane < 2 * SUB, packed, pltpu.roll(right[rows:], 2 * SUB, 1))
-    out_0[pl.ds(SUB, SUB), :] = packed
-    out_1[pl.ds(SUB, SUB), :] = packed
-    for copy in copies:
-        copy.wait()
-    spots = (jnp.where(lat_even, 2, 0), 1, jnp.where(lat_even, 0, 2))
-    for n, da in enumerate(NEAR):
-        number = lambda kind, o: params[spots[n], kind, o]
-        for o in range(SUB):
-            total = share(pad, number, rows, cols, da, 0, o)
-            row = number(AT_ROW, o).astype(jnp.int32) - 1 + da * rows
-            row = jnp.clip(row, -2, rows) + SUB
-            col = number(AT_COL, o).astype(jnp.int32)
-            for side, at in enumerate((0, cols)):
-                for k in (side, side + 2):
-                    weight = jnp.where(col == at, number(k, o), 0.0)
-                    total = total + weight * sides[side, pl.ds(row + k // 2, 1), :]
-            block[n, pl.ds(o, 1), :] = total
-    own_ref[...] = block[1] - own_shift(lambda kind, o: params[1, kind, o])
-    out_0[pl.ds(0, SUB), :] = jnp.where(lat_even, block[2], block[0])
-    out_1[pl.ds(0, SUB), :] = jnp.where(lat_even, block[0], block[2])
-
-
-def block_kernel(own, ends_0, ends_1, out_ref):
-    part = pl.ds(0, SUB)
-    value = own[...] + ends_0[part, :] + ends_1[part, :]
+def send_block(value, out_ref):
     mean = jnp.mean(value, axis=-1, keepdims=True)
     innov = jnp.broadcast_to(-mean, value.shape)
     block = jnp.concatenate([value - mean, innov], axis=0).astype(BF16)
     out_ref[...] = jnp.broadcast_to(block, out_ref.shape)
 
 
-def later_kernel(mine, sides_0, sides_1, ends_0, ends_1, pad, out_ref, params, sems):
+def prior_kernel(mine, *refs):
+    came, (pad, out_ref, ends, sides, corners, value, params, sem) = (refs[:8], refs[8:])
     rows, cols = (pad.shape[0] - 4, pad.shape[1] - 2 * SUB)
+    copy = pltpu.make_async_copy(mine.at[0], params, sem)
+    copy.start()
     lon_even, lat_even = (is_even("lon"), is_even("lat"))
-    side, end = (pl.ds(rows, SUB), pl.ds(SUB, SUB))
-    sources = (sides_0.at[side], mine.at[1], sides_1.at[side], ends_0.at[end], ends_1.at[end])
+    held = dict(zip(TRADES, came))
+    first, second = (held[0, None][pl.ds(0, cols), :], held[1, None][pl.ds(0, cols), :])
+    ends[0, pl.ds(SUB, cols), :] = jnp.where(lat_even, second, first)
+    ends[1, pl.ds(SUB, cols), :] = jnp.where(lat_even, first, second)
+    first, second = (held[None, 0][pl.ds(0, rows), :], held[None, 1][pl.ds(0, rows), :])
+    sides[...] = jnp.zeros_like(sides)
+    sides[0, pl.ds(SUB, rows), :] = jnp.where(lon_even, second, first)
+    sides[1, pl.ds(SUB, rows), :] = jnp.where(lon_even, first, second)
+    for lat_kind in range(2):
+        for lon_kind in range(2):
+            corners[2 * lat_kind + lon_kind] = held[lat_kind, lon_kind][pl.ds(0, SUB), :]
+    for end, da in enumerate((-1, 1)):
+        for side, dc in enumerate((-1, 1)):
+            corner = corners[2 * kind_at("lat", da) + kind_at("lon", dc)]
+            ends[end, pl.ds(side * (cols + SUB), SUB), :] = corner
+    copy.wait()
+    number = lambda kind, o: params[kind, o]
+    for o in range(SUB):
+        total = share(pad, number, rows, cols, 0, 0, o)
+        row = number(AT_ROW, o).astype(jnp.int32)
+        col = number(AT_COL, o).astype(jnp.int32)
+        for n, at in enumerate((0, rows)):
+            for k in range(2):
+                weight = jnp.where(row == at, number(2 * n + k, o), 0.0)
+                total = total + weight * ends[n, pl.ds(col + SUB - 1 + k, 1), :]
+        for n, at in enumerate((0, cols)):
+            for k in range(2):
+                weight = jnp.where(col == at, number(n + 2 * k, o), 0.0)
+                total = total + weight * sides[n, pl.ds(row + SUB - 1 + k, 1), :]
+        value[pl.ds(o, 1), :] = total
+    send_block(value[...] - own_shift(number), out_ref)
+
+
+def meet_kernel(own, *refs):
+    total = own[...]
+    for share_ref in refs[:-1]:
+        total = total + share_ref[...]
+    send_block(total, refs[-1])
+
+
+def later_kernel(mine, *refs):
+    came, (pad, out_ref, params, sems) = (refs[:8], refs[8:])
+    rows, cols = (pad.shape[0] - 4, pad.shape[1] - 2 * SUB)
+    sources = [block.at[pl.ds(block.shape[0] - SUB, SUB)] for block in came] + [mine.at[1]]
     copies = []
     for n, source in enumerate(sources):
         copies.append(pltpu.make_async_copy(source, params.at[n], sems.at[n]))
         copies[-1].start()
     for copy in copies:
         copy.wait()
-    beside = (jnp.where(lon_even, 2, 0), 1, jnp.where(lon_even, 0, 2))
-    above = (jnp.where(lat_even, 4, 3), None, jnp.where(lat_even, 3, 4))
-    for n, dc in enumerate(NEAR):
-        for m, da in enumerate(NEAR):
-            if da == 0:
-                number = lambda kind, o: params[beside[n], kind, o]
-            else:
-                number = lambda kind, o: params[above[m], kind, n * SUB + o]
-            for o in range(SUB):
-                at = (n * len(NEAR) + m) * SUB + o
-                out_ref[pl.ds(at, 1), :] = share(pad, number, rows, cols, da, dc, o)
-    out_ref[pl.ds(len(NEAR) ** 2 * SUB, SUB), :] = own_shift(lambda kind, o: params[1, kind, o])
+    for n, (dc, da) in enumerate(AROUND):
+        if da == 0 and dc == 0:
+            spot = len(TRADES)
+        elif dc == 0:
+            spot = TRADES.index((0, None)) + kind_at("lat", da)
+        elif da == 0:
+            spot = TRADES.index((None, 0)) + kind_at("lon", dc)
+        else:
+            spot = TRADES.index((0, 0)) + 2 * kind_at("lat", da) + kind_at("lon", dc)
+        number = lambda kind, o: params[spot, kind, o]
+        for o in range(SUB):
+            out_ref[n, pl.ds(o, 1), :] = share(pad, number, rows, cols, da, dc, o)
+    out_ref[len(AROUND)] = own_shift(lambda kind, o: params[len(TRADES), kind, o])
 
 
 def window_start(lat_count, my_lat):
@@ -270,46 +309,31 @@
     )
 
 
-def first_kernel(batch, lat_count, near_ref, pattern_ref, later, mid_ref, out_0, out_1, map_ref):
+def first_kernel(batch, lat_count, near_ref, pattern_ref, later, map_ref, own_ref, *refs):
+    outs, moved = (refs[:-1], refs[-1])
     flipped = batch_map(batch, lat_count, near_ref, pattern_ref)
     map_ref[...] = flipped
-    size = len(NEAR) * SUB
-    moved = exact_dot(later[pl.ds(0, len(NEAR) * size), :], flipped, 1)
-    left, right = (moved[:size], moved[2 * size:])
-    even = is_even("lon")
-    out_0[...] = jnp.where(even, right, left)
-    out_1[...] = jnp.where(even, left, right)
-    mid_ref[...] = moved[size:2 * size]
-    own = pl.ds(SUB, SUB)
-    mid_ref[own, :] = mid_ref[own, :] - later[pl.ds(len(NEAR) * size, SUB), :]
-
-
-def meet_kernel(mid, sides_0, sides_1, own_ref, out_0, out_1):
-    total = mid[...] + sides_0[...] + sides_1[...]
-    above, own_ref[...], below = (total[:SUB], total[SUB:2 * SUB], total[2 * SUB:])
-    even = is_even("lat")
-    out_0[...] = jnp.where(even, below, above)
-    out_1[...] = jnp.where(even, above, below)
-
-
-def last_kernel(
-    batch, lat_count, near_ref, pattern_ref, map_ref, cells_ref, out_ref, cells, result, cell_sem, out_sem
-):
+    count = len(AROUND)
+    moved[...] = exact_dot(later[pl.ds(0, count)].reshape(-1, LANES), flipped, 1).reshape(moved.shape)
+    own_ref[...] = moved[AROUND.index((0, 0))] - later[count]
+    for (lat_kind, lon_kind), out in zip(TRADES, outs):
+        out[...] = moved[(toward("lon", lon_kind) + 1) * len(NEAR) + toward("lat", lat_kind) + 1]
+
+
+def last_kernel(batch, lat_count, near_ref, pattern_ref, map_ref, pad, out_ref, result, out_sem):
     parts = out_sem.shape[0]
-    rows = cells.shape[0] // parts
-    copy = pltpu.make_async_copy(cells_ref, cells, cell_sem)
-    copy.start()
+    rows, cols = (pad.shape[0] - 4, pad.shape[1] - 2 * SUB)
     flipped = exact_dot(batch_map(batch, lat_count, near_ref, pattern_ref), map_ref[...], 0)
     high = flipped.astype(BF16)
     low = (flipped - high.astype(F32)).astype(BF16)
     right = jnp.concatenate(
         [jnp.concatenate([high, high], axis=1), jnp.concatenate([low, jnp.zeros_like(low)], axis=1)], axis=0
     )
-    copy.wait()
     copies = []
+    size = rows // parts
     for n in range(parts):
-        part = pl.ds(n * rows, rows)
-        value = cells[part, :]
+        part = pl.ds(n * size * cols, size * cols)
+        value = pad[pl.ds(2 + n * size, size), pl.ds(SUB, cols), :].reshape(size * cols, LANES)
         upper = value.astype(BF16)
         rest = (value - upper.astype(F32)).astype(BF16)
         both = lax.dot_general(
@@ -335,7 +359,6 @@
     batches = observed.shape[0]
     lat_count, lon_count = (lax.axis_size("lat"), lax.axis_size("lon"))
     tiles = lat_count * lon_count
-    column = len(NEAR) * SUB
     vmem = pl.BlockSpec(memory_space=pltpu.VMEM)
     smem = pl.BlockSpec(memory_space=pltpu.SMEM)
     anywhere = pl.BlockSpec(memory_space=pl.ANY)
@@ -356,97 +379,82 @@
             name=name,
         )(*operands)
 
-    def trade(blocks, axis):
-        count, wraps = ((lon_count, True) if axis == "lon" else (lat_count, False))
-        second = swap(blocks[1], axis, 1, count, wraps)
-        first = swap(blocks[0], axis, 0, count, wraps)
-        return (first, second)
-
-    def gathered(own, ends):
-        block = shape(tiles, 2 * SUB, members, dtype=BF16)
-        blocks = call(block_kernel, "own_block", [vmem] * 3, block, [], own, *ends)
+    def exchange(blocks):
         blocks = lax.all_to_all(blocks, ("lat", "lon"), split_axis=0, concat_axis=0, tiled=True)
         return window(blocks, lat_count, lon_count)
 
     small = (observed, precision, interp_weight, stencil, owned)
-    side = shape(rows + SUB, members)
-    mine, *sides = call(
+    sizes = [rows if lat is None else cols if lon is None else SUB for lat, lon in TRADES]
+    mine, *edges = call(
         functools.partial(start_kernel, cols + 2),
         "start",
         [hbm] * 6,
-        (shape(batches, SUB, LANES), side, side),
+        (shape(batches, SUB, LANES),) + tuple(shape(size + SUB, members) for size in sizes),
         [pltpu.VMEM(array.shape, array.dtype) for array in small]
-        + [pltpu.VMEM((rows, SUB, members), F32)] * 2
-        + [pltpu.SemaphoreType.DMA((7,))],
+        + [pltpu.VMEM((2, rows, SUB, members), F32), pltpu.VMEM((2, cols, members), F32)]
+        + [pltpu.SemaphoreType.DMA((9,))],
         *small,
         ensemble,
         limit=63,
     )
-    sides = trade(sides, "lon")
-    ends = trade((mine[0], mine[0]), "lat")
+    edges = trade(edges, lat_count, lon_count)
     padded = shape(rows + 4, cols + 2 * SUB, members)
     pad = call(pad_kernel, "pad", [hbm], padded, [pltpu.SemaphoreType.DMA], ensemble)
-    end = shape(2 * SUB, members)
-    own, *ends = call(
-        column_kernel,
-        "column_shares",
-        [vmem] * 6,
-        (shape(SUB, members), end, end),
+    slots = shape(tiles, 2 * SUB, members, dtype=BF16)
+    blocks = call(
+        prior_kernel,
+        "prior",
+        [vmem] * 10,
+        slots,
         [
-            pltpu.VMEM((3, SUB, members), F32),
+            pltpu.VMEM((2, cols + 2 * SUB, members), F32),
             pltpu.VMEM((2, rows + 2 * SUB, members), F32),
-            pltpu.SMEM((3, SUB, LANES), F32),
-            pltpu.SemaphoreType.DMA((3,)),
+            pltpu.VMEM((4, SUB, members), F32),
+            pltpu.VMEM((SUB, members), F32),
+            pltpu.SMEM((SUB, LANES), F32),
+            pltpu.SemaphoreType.DMA,
         ],
         mine,
-        *sides,
-        *ends,
+        *edges,
         pad,
     )
-    ends = trade(ends, "lat")
-    near = gathered(own, ends)
+    near = exchange(blocks)
+    count = len(AROUND)
     later = call(
         later_kernel,
         "later_shares",
-        [vmem] * 6,
-        shape(len(NEAR) * column + SUB, members),
-        [pltpu.SMEM((5, SUB, LANES), F32), pltpu.SemaphoreType.DMA((5,))],
+        [vmem] * 10,
+        shape(count + 1, SUB, members),
+        [pltpu.SMEM((count, SUB, LANES), F32), pltpu.SemaphoreType.DMA((count,))],
         mine,
-        *sides,
-        *ends,
+        *edges,
         pad,
     )
-    part = shape(column, members)
-    mid, first, second, first_map = call(
+    block = shape(SUB, members)
+    first_map, own, *shares = call(
         functools.partial(first_kernel, 0, lat_count),
         "first_batch",
         [vmem, smem, vmem],
-        (part, part, part, shape(members, members)),
-        [],
+        (shape(members, members),) + (block,) * count,
+        [pltpu.VMEM((count, SUB, members), F32)],
         near,
         pattern,
         later,
     )
-    sides = trade((first, second), "lon")
-    block = shape(SUB, members)
-    own, *ends = call(meet_kernel, "meet", [vmem] * 3, (block, block, block), [], mid, *sides)
-    near = gathered(own, trade(ends, "lat"))
+    shares = trade(shares, lat_count, lon_count)
+    blocks = call(meet_kernel, "own_block", [vmem] * count, slots, [], own, *shares)
+    near = exchange(blocks)
     parts = 8
     result = call(
         functools.partial(last_kernel, 1, lat_count),
         "second_batch",
-        [vmem, smem, vmem, anywhere],
+        [vmem, smem, vmem, vmem],
         shape(rows * cols, members),
-        [
-            pltpu.VMEM((rows * cols, members), F32),
-            pltpu.VMEM((rows * cols, members), F32),
-            pltpu.SemaphoreType.DMA,
-            pltpu.SemaphoreType.DMA((parts,)),
-        ],
+        [pltpu.VMEM((rows * cols, members), F32), pltpu.SemaphoreType.DMA((parts,))],
         near,
         pattern,
         first_map,
-        ensemble.reshape(rows * cols, members),
+        pad,
         out_specs=anywhere,
     )
     return result.reshape(rows, cols, members)

time: 67.8 us -> 80.1 us (1.18)
  starting transfers between devices: 19.1 us -> 32.2 us
  waiting for transfers between devices: 13.3 us -> 8.06 us
  blocking collectives: 12.3 us -> 17.5 us
  local copies, waits for them, and re-layouts: 3.93 us -> 2.02 us
  Pallas kernels: 18.7 us -> 19.7 us
    ppermute x10 -> x16, starting transfers between devices: 13.6 us -> 21.2 us  [trade(): results.append(lax.ppermute(block, ('lat', 'lon'), route))]
    all_to_all x1, starting transfers between devices: 5.45 us -> 11.1 us  [exchange(): lax.all_to_all(blocks, ('lat', 'lon'), split_axis=0, concat_axis=0, tiled...]
    all_to_all x1, blocking collectives: 12.3 us -> 17.5 us  [exchange(): lax.all_to_all(blocks, ('lat', 'lon'), split_axis=0, concat_axis=0, tiled...]
    ppermute x10 -> x16, waiting for transfers between devices: 6.67 us -> 1.78 us  [trade(): results.append(lax.ppermute(block, ('lat', 'lon'), route))]
    unnamed x9 -> x7, local copies, waits for them, and re-layouts: 3.19 us -> 2.02 us
    pallas_call x9 -> x7, Pallas kernels: 18.7 us -> 19.7 us  [call(): pl.pallas_call(kernel, out_shape=out_shape, in_specs=specs, out_specs=out...]
  transfers between devices with their start and end apart: 11 -> 17, of which waited for: 5 -> 3; matrix products, arithmetic and copies ran while one was open for 1% -> 0% of each run, Pallas kernels for 3% -> 3%
where the time goes in v3:
time: 80.1 us; the launch traced here: 79.7 us
  starting transfers between devices  32.2 us (40%)
  Pallas kernels  19.7 us (25%)
  blocking collectives  17.5 us (22%)
  waiting for transfers between devices  8.06 us (10%)
  local copies, waits for them, and re-layouts  2.02 us (3%)
    ppermute x16, starting transfers between devices, trade(): results.append(lax.ppermute(block, ('lat', 'lon'), route))  21.2 us
    pallas_call x7, Pallas kernels, call(): pl.pallas_call(kernel, out_shape=out_shape, in_specs=specs, out_specs=out...  19.7 us
    all_to_all x1, blocking collectives, exchange(): lax.all_to_all(blocks, ('lat', 'lon'), split_axis=0, concat_axis=0, tiled...  17.5 us
    all_to_all x1, starting transfers between devices, exchange(): lax.all_to_all(blocks, ('lat', 'lon'), split_axis=0, concat_axis=0, tiled...  11.1 us
    all_to_all x1, waiting for transfers between devices, exchange(): lax.all_to_all(blocks, ('lat', 'lon'), split_axis=0, concat_axis=0, tiled...  6.28 us
    unnamed x7, local copies, waits for them, and re-layouts  2.02 us
    ppermute x16, waiting for transfers between devices, trade(): results.append(lax.ppermute(block, ('lat', 'lon'), route))  1.78 us
  transfers between devices with their start and end apart: 17, of which 3 were waited for; matrix products, arithmetic and copies ran while one was open for 0% of the time, Pallas kernels for 3%

profile of v3, /device:TPU:0, one launch (start us, length us, event | category | flops | bytes accessed | tf_op | source)
XLA Modules:
  0.0 79.7 jit_solution(5946263170223665761)
XLA Ops:
  0.0 1.9 %start.1 = (f32[2,8,128]{2,1,0:T(8,128)}, f32[136,128]{1,0:T(8,128)}, f32[136,128]{1,0:T(8,128)}, f32[40,128]{1,0:T(8,128)}, f32[40,128]{1,0:T(8,128)}, /*index=...) custom-call(f32[2,1,1,8]{3,2,1,0:T(1,128)} %observed.1, f32[2,1,1,8]{3,2,1,0:T(1,128)} %precision.1, ...), custom_call_target="tpu_custom_call" | custom-call | tf_op jit(solution)/shard_map/start/pallas_call | solution.py:372
  1.9 3.1 %collective-permute-start = (f32[136,128]{1,0:T(8,128)}, f32[136,128]{1,0:T(8,128)S(1)}, u32[]{:S(2)}, u32[]{:S(2)}) collective-permute-start(f32[136,128]{1,0:T(8,128)} %get-tuple-element.25), channel_id=1, source_target_pairs={{0,8},{1,9},{2,10},{3,11},{4,12},{5,13},{6,14},{7,15},{8,0},{9,1},... | collective-permute-start | bytes 208904 | tf_op jit(solution)/shard_map/ppermute | solution.py:35
  5.0 0.7 collective-permute-start.1
  5.6 3.3 %collective-permute-start.4 = (f32[16,128]{1,0:T(8,128)}, f32[16,128]{1,0:T(8,128)S(1)}, u32[]{:S(2)}, u32[]{:S(2)}) collective-permute-start(f32[16,128]{1,0:T(8,128)} %get-tuple-element.29), channel_id=1, source_target_pairs={{0,9},{1,8},{2,11},{3,10},{4,13},{5,12},{6,15},{7,14},{8,1},{9,0},... | collective-permute-start | bytes 24584 | tf_op jit(solution)/shard_map/ppermute | solution.py:35
  9.0 2.0 %collective-permute-start.5 = (f32[16,128]{1,0:T(8,128)}, f32[16,128]{1,0:T(8,128)S(1)}, u32[]{:S(2)}, u32[]{:S(2)}) collective-permute-start(f32[16,128]{1,0:T(8,128)} %get-tuple-element.30), channel_id=1, source_target_pairs={{0,15},{1,10},{2,9},{3,12},{4,11},{5,14},{6,13},{7,8},{8,7},{9,2},... | collective-permute-start | bytes 24584 | tf_op jit(solution)/shard_map/ppermute | solution.py:35
  10.9 0.3 collective-permute-start.2
  11.2 0.0 collective-permute-done.4.refs_4_
  11.2 2.6 %collective-permute-start.3 = (f32[40,128]{1,0:T(8,128)}, f32[40,128]{1,0:T(8,128)S(1)}, u32[]{:S(2)}, u32[]{:S(2)}) collective-permute-start(f32[40,128]{1,0:T(8,128)} %get-tuple-element.28), channel_id=1, source_target_pairs={{0,7},{1,2},{2,1},{3,4},{4,3},{5,6},{6,5},{7,0},{8,15},{9,10},{10,... | collective-permute-start | bytes 61448 | tf_op jit(solution)/shard_map/ppermute | solution.py:35
  13.8 0.3 collective-permute-done.5.refs_5_
  14.0 0.7 collective-permute-start.6
  14.7 0.0 collective-permute-done.6.refs_6_
  14.7 0.7 collective-permute-start.7
  15.4 0.0 copy-start
  15.4 1.6 %copy-done = f32[32,128,128]{2,1,0:T(8,128)S(1)} copy-done((f32[32,128,128]{2,1,0:T(8,128)S(1)}, f32[32,128,128]{2,1,0:T(8,128)}, u32[]{:S(2)}) %copy-start) | copy-done | bytes 2097176
  17.0 0.0 copy-start.1
  17.0 0.2 pad.1.refs_8_
  17.2 0.0 copy-start.2
  17.2 0.0 collective-permute-done.7.refs_7_
  17.2 0.0 collective-permute-done.2.refs_2_
  17.2 0.0 collective-permute-done.3.refs_3_
  17.2 0.0 collective-permute-done.refs_0_
  17.2 0.0 collective-permute-done.1.refs_1_
  17.2 0.4 copy-done.1
  17.7 1.5 %prior.1 = bf16[32,16,128]{2,1,0:T(8,128)(2,1)} custom-call(f32[2,8,128]{2,1,0:T(8,128)S(1)} %copy-done.1, f32[136,128]{1,0:T(8,128)S(1)} %collective-permute-done.refs_0_, f32[136,128]{1,0:T(8,128)S(1)} %collective-permute-done.1.refs_1_, f32[40,128]{1,0:T(8,128)S(1)} %collective-permute-done.2.refs_2_, f32[40,128]{1,0:T(8,128)S(1)} %collective-permute-done.3.refs_3_, ...), custom_call_target="tpu_custom_call" | custom-call | tf_op jit(solution)/shard_map/prior/pallas_call | solution.py:372
  19.1 11.1 %all-to-all-start = ((bf16[32,16,128]{2,1,0:T(8,128)(2,1)}), bf16[32,16,128]{2,1,0:T(8,128)(2,1)S(1)}, u32[]{:S(2)}, u32[]{:S(2)}) async-start(bf16[32,16,128]{2,1,0:T(8,128)(2,1)} %prior.1), calls=%async_computation | async-start | bytes 262144 | tf_op jit(solution)/shard_map/all_to_all | solution.py:383
  30.2 0.0 copy-done.2
  30.2 1.9 %later_shares.1.later = f32[10,8,128]{2,1,0:T(8,128)S(1)} custom-call(f32[2,8,128]{2,1,0:T(8,128)S(1)} %copy-done.1, f32[136,128]{1,0:T(8,128)S(1)} %collective-permute-done.refs_0_, f32[136,128]{1,0:T(8,128)S(1)} %collective-permute-done.1.refs_1_, f32[40,128]{1,0:T(8,128)S(1)} %collective-permute-done.2.refs_2_, ...), custom_call_target="tpu_custom_call" | custom-call | tf_op jit(solution)/shard_map/later_shares/pallas_call | solution.py:372
  32.2 6.3 %all-to-all-done.near_ref = bf16[32,16,128]{2,1,0:T(8,128)(2,1)S(1)} async-done(((bf16[32,16,128]{2,1,0:T(8,128)(2,1)}), bf16[32,16,128]{2,1,0:T(8,128)(2,1)S(1)}, u32[]{:S(2)}, u32[]{:S(2)}) %all-to-all-start) | async-done | bytes 131104 | tf_op jit(solution)/shard_map/all_to_all | solution.py:383
  38.4 5.7 %first_batch.1 = (f32[128,128]{1,0:T(8,128)S(1)}, f32[8,128]{1,0:T(8,128)S(1)}, f32[8,128]{1,0:T(8,128)S(1)}, f32[8,128]{1,0:T(8,128)S(1)}, f32[8,128]{1,0:T(8,1...) custom-call(bf16[32,16,128]{2,1,0:T(8,128)(2,1)S(1)} %all-to-all-don, ...), custom_call_target="tpu_custom_call" | custom-call | tf_op jit(solution)/shard_map/first_batch/pallas_call | solution.py:372
  44.2 0.7 collective-permute-start.8
  44.9 0.6 collective-permute-start.9
  45.6 0.1 collective-permute-start.10
  45.6 1.0 %collective-permute-start.11 = (f32[8,128]{1,0:T(8,128)S(1)}, f32[8,128]{1,0:T(8,128)S(1)}, u32[]{:S(2)}, u32[]{:S(2)}) collective-permute-start(f32[8,128]{1,0:T(8,128)S(1)} %get-tuple-element.37), channel_id=1, source_target_pairs={{0,7},{1,2},{2,1},{3,4},{4,3},{5,6},{6,5},{7,0},{8,15},{9,10},{10,... | collective-permute-start | bytes 12296 | tf_op jit(solution)/shard_map/ppermute | solution.py:35
  46.6 2.2 %collective-permute-start.12 = (f32[8,128]{1,0:T(8,128)S(1)}, f32[8,128]{1,0:T(8,128)S(1)}, u32[]{:S(2)}, u32[]{:S(2)}) collective-permute-start(f32[8,128]{1,0:T(8,128)S(1)} %get-tuple-element.38), channel_id=1, source_target_pairs={{0,9},{1,8},{2,11},{3,10},{4,13},{5,12},{6,15},{7,14},{8,1},{9,0},... | collective-permute-start | bytes 12296 | tf_op jit(solution)/shard_map/ppermute | solution.py:35
  48.9 0.0 collective-permute-done.8.refs_0_
  48.9 2.0 %collective-permute-start.13 = (f32[8,128]{1,0:T(8,128)S(1)}, f32[8,128]{1,0:T(8,128)S(1)}, u32[]{:S(2)}, u32[]{:S(2)}) collective-permute-start(f32[8,128]{1,0:T(8,128)S(1)} %get-tuple-element.39), channel_id=1, source_target_pairs={{0,15},{1,10},{2,9},{3,12},{4,11},{5,14},{6,13},{7,8},{8,7},{9,2},... | collective-permute-start | bytes 12296 | tf_op jit(solution)/shard_map/ppermute | solution.py:35
  50.8 0.0 collective-permute-done.9.refs_1_
  50.8 0.7 collective-permute-start.14
  51.5 0.0 collective-permute-done.10.refs_2_
  51.5 0.7 collective-permute-start.15
  52.2 0.0 collective-permute-done.11.refs_3_
  52.2 0.0 collective-permute-done.12.refs_4_
  52.2 1.5 %collective-permute-done.13.refs_5_ = f32[8,128]{1,0:T(8,128)S(1)} collective-permute-done((f32[8,128]{1,0:T(8,128)S(1)}, f32[8,128]{1,0:T(8,128)S(1)}, u32[]{:S(2)}, u32[]{:S(2)}) %collective-permute-start.13) | collective-permute-done | bytes 4128 | tf_op jit(solution)/shard_map/ppermute | solution.py:35
  53.7 0.0 collective-permute-done.14.refs_6_
  53.7 0.0 collective-permute-done.15.refs_7_
  53.7 0.1 own_block.1
  53.8 17.5 %all_to_all.10.near_ref = bf16[32,16,128]{2,1,0:T(8,128)(2,1)S(1)} all-to-all(bf16[32,16,128]{2,1,0:T(8,128)(2,1)S(1)} %own_block.1), channel_id=1, replica_groups=mesh['lat'=4,'lon'=8] {'lat','lon'}, dimensions={0} | all-to-all | bytes 262144 | tf_op jit(solution)/shard_map/all_to_all | solution.py:383
  71.3 8.4 %second_batch.1 = f32[4096,128]{1,0:T(8,128)} custom-call(bf16[32,16,128]{2,1,0:T(8,128)(2,1)S(1)} %all_to_all.10.near_ref, s32[2,1,1,5,8]{4,3,2,1,0:T(8,128)S(1)} %copy.8.pattern_ref, f32[128,128]{1,0:T(8,128)S(1)} %get-tuple-element.42.map_ref, f32[36,144,128]{2,1,0:T(8,128)S(1)} %pad.1.refs_8_), custom_call_target="tpu_custom_call" | custom-call | tf_op jit(solution)/shard_map/second_batch/pallas_call | solution.py:372
  (1 shorter events, 0.0 us)
Async XLA Ops:
  1.9 15.4 %collective-permute-start = (f32[136,128]{1,0:T(8,128)}, f32[136,128]{1,0:T(8,128)S(1)}, u32[]{:S(2)}, u32[]{:S(2)}) collective-permute-start(f32[136,128]{1,0:T(8,128)} %get-tuple-element.25), channel_id=1, source_target_pairs={{0,8},{1,9},{2,10},{3,11},{4,12},{5,13},{6,14},{7,15},{8,0},{9,1},... | collective-permute-start | bytes 208904 | tf_op jit(solution)/shard_map/ppermute | solution.py:35
  5.0 12.3 %collective-permute-start.1 = (f32[136,128]{1,0:T(8,128)}, f32[136,128]{1,0:T(8,128)S(1)}, u32[]{:S(2)}, u32[]{:S(2)}) collective-permute-start(f32[136,128]{1,0:T(8,128)} %get-tuple-element.26), channel_id=1, source_target_pairs={{8,16},{9,17},{10,18},{11,19},{12,20},{13,21},{14,22},{15,23},{16,... | collective-permute-start | bytes 208904 | tf_op jit(solution)/shard_map/ppermute | solution.py:35
  5.6 5.6 %collective-permute-start.4 = (f32[16,128]{1,0:T(8,128)}, f32[16,128]{1,0:T(8,128)S(1)}, u32[]{:S(2)}, u32[]{:S(2)}) collective-permute-start(f32[16,128]{1,0:T(8,128)} %get-tuple-element.29), channel_id=1, source_target_pairs={{0,9},{1,8},{2,11},{3,10},{4,13},{5,12},{6,15},{7,14},{8,1},{9,0},... | collective-permute-start | bytes 24584 | tf_op jit(solution)/shard_map/ppermute | solution.py:35
  9.0 5.1 %collective-permute-start.5 = (f32[16,128]{1,0:T(8,128)}, f32[16,128]{1,0:T(8,128)S(1)}, u32[]{:S(2)}, u32[]{:S(2)}) collective-permute-start(f32[16,128]{1,0:T(8,128)} %get-tuple-element.30), channel_id=1, source_target_pairs={{0,15},{1,10},{2,9},{3,12},{4,11},{5,14},{6,13},{7,8},{8,7},{9,2},... | collective-permute-start | bytes 24584 | tf_op jit(solution)/shard_map/ppermute | solution.py:35
  10.9 6.3 %collective-permute-start.2 = (f32[40,128]{1,0:T(8,128)}, f32[40,128]{1,0:T(8,128)S(1)}, u32[]{:S(2)}, u32[]{:S(2)}) collective-permute-start(f32[40,128]{1,0:T(8,128)} %get-tuple-element.27), channel_id=1, source_target_pairs={{0,1},{1,0},{2,3},{3,2},{4,5},{5,4},{6,7},{7,6},{8,9},{9,8},{10,11... | collective-permute-start | bytes 61448 | tf_op jit(solution)/shard_map/ppermute | solution.py:35
  11.2 6.0 %collective-permute-start.3 = (f32[40,128]{1,0:T(8,128)}, f32[40,128]{1,0:T(8,128)S(1)}, u32[]{:S(2)}, u32[]{:S(2)}) collective-permute-start(f32[40,128]{1,0:T(8,128)} %get-tuple-element.28), channel_id=1, source_target_pairs={{0,7},{1,2},{2,1},{3,4},{4,3},{5,6},{6,5},{7,0},{8,15},{9,10},{10,... | collective-permute-start | bytes 61448 | tf_op jit(solution)/shard_map/ppermute | solution.py:35
  14.0 0.7 collective-permute-start.6
  14.7 2.5 %collective-permute-start.7 = (f32[16,128]{1,0:T(8,128)}, f32[16,128]{1,0:T(8,128)S(1)}, u32[]{:S(2)}, u32[]{:S(2)}) collective-permute-start(f32[16,128]{1,0:T(8,128)} %get-tuple-element.32), channel_id=1, source_target_pairs={{8,23},{9,18},{10,17},{11,20},{12,19},{13,22},{14,21},{15,16},{16,... | collective-permute-start | bytes 24584 | tf_op jit(solution)/shard_map/ppermute | solution.py:35
  15.4 1.6 %copy-start = (f32[32,128,128]{2,1,0:T(8,128)S(1)}, f32[32,128,128]{2,1,0:T(8,128)}, u32[]{:S(2)}) copy-start(f32[32,128,128]{2,1,0:T(8,128)} %cells.3) | copy-start | bytes 6291460
  17.0 0.7 copy-start.1
  17.2 13.0 %copy-start.2 = (s32[2,1,1,5,8]{4,2,3,1,0:T(1,128)S(1)}, s32[2,1,1,5,8]{4,2,3,1,0:T(1,128)}, u32[]{:S(2)}) copy-start(s32[2,1,1,5,8]{4,2,3,1,0:T(1,128)} %param.13) | copy-start | bytes 964
  19.1 19.3 %all-to-all-start = ((bf16[32,16,128]{2,1,0:T(8,128)(2,1)}), bf16[32,16,128]{2,1,0:T(8,128)(2,1)S(1)}, u32[]{:S(2)}, u32[]{:S(2)}) async-start(bf16[32,16,128]{2,1,0:T(8,128)(2,1)} %prior.1), calls=%async_computation | async-start | bytes 262144 | tf_op jit(solution)/shard_map/all_to_all | solution.py:383
  44.2 4.7 %collective-permute-start.8 = (f32[8,128]{1,0:T(8,128)S(1)}, f32[8,128]{1,0:T(8,128)S(1)}, u32[]{:S(2)}, u32[]{:S(2)}) collective-permute-start(f32[8,128]{1,0:T(8,128)S(1)} %get-tuple-element.34), channel_id=1, source_target_pairs={{0,8},{1,9},{2,10},{3,11},{4,12},{5,13},{6,14},{7,15},{8,0},{9,1},... | collective-permute-start | bytes 12296 | tf_op jit(solution)/shard_map/ppermute | solution.py:35
  44.9 5.9 %collective-permute-start.9 = (f32[8,128]{1,0:T(8,128)S(1)}, f32[8,128]{1,0:T(8,128)S(1)}, u32[]{:S(2)}, u32[]{:S(2)}) collective-permute-start(f32[8,128]{1,0:T(8,128)S(1)} %get-tuple-element.35), channel_id=1, source_target_pairs={{8,16},{9,17},{10,18},{11,19},{12,20},{13,21},{14,22},{15,23},{16,... | collective-permute-start | bytes 12296 | tf_op jit(solution)/shard_map/ppermute | solution.py:35
  45.6 6.0 %collective-permute-start.10 = (f32[8,128]{1,0:T(8,128)S(1)}, f32[8,128]{1,0:T(8,128)S(1)}, u32[]{:S(2)}, u32[]{:S(2)}) collective-permute-start(f32[8,128]{1,0:T(8,128)S(1)} %get-tuple-element.36), channel_id=1, source_target_pairs={{0,1},{1,0},{2,3},{3,2},{4,5},{5,4},{6,7},{7,6},{8,9},{9,8},{10,11... | collective-permute-start | bytes 12296 | tf_op jit(solution)/shard_map/ppermute | solution.py:35
  45.6 6.6 %collective-permute-start.11 = (f32[8,128]{1,0:T(8,128)S(1)}, f32[8,128]{1,0:T(8,128)S(1)}, u32[]{:S(2)}, u32[]{:S(2)}) collective-permute-start(f32[8,128]{1,0:T(8,128)S(1)} %get-tuple-element.37), channel_id=1, source_target_pairs={{0,7},{1,2},{2,1},{3,4},{4,3},{5,6},{6,5},{7,0},{8,15},{9,10},{10,... | collective-permute-start | bytes 12296 | tf_op jit(solution)/shard_map/ppermute | solution.py:35
  46.6 5.5 %collective-permute-start.12 = (f32[8,128]{1,0:T(8,128)S(1)}, f32[8,128]{1,0:T(8,128)S(1)}, u32[]{:S(2)}, u32[]{:S(2)}) collective-permute-start(f32[8,128]{1,0:T(8,128)S(1)} %get-tuple-element.38), channel_id=1, source_target_pairs={{0,9},{1,8},{2,11},{3,10},{4,13},{5,12},{6,15},{7,14},{8,1},{9,0},... | collective-permute-start | bytes 12296 | tf_op jit(solution)/shard_map/ppermute | solution.py:35
  48.9 4.8 %collective-permute-start.13 = (f32[8,128]{1,0:T(8,128)S(1)}, f32[8,128]{1,0:T(8,128)S(1)}, u32[]{:S(2)}, u32[]{:S(2)}) collective-permute-start(f32[8,128]{1,0:T(8,128)S(1)} %get-tuple-element.39), channel_id=1, source_target_pairs={{0,15},{1,10},{2,9},{3,12},{4,11},{5,14},{6,13},{7,8},{8,7},{9,2},... | collective-permute-start | bytes 12296 | tf_op jit(solution)/shard_map/ppermute | solution.py:35
  50.8 2.9 %collective-permute-start.14 = (f32[8,128]{1,0:T(8,128)S(1)}, f32[8,128]{1,0:T(8,128)S(1)}, u32[]{:S(2)}, u32[]{:S(2)}) collective-permute-start(f32[8,128]{1,0:T(8,128)S(1)} %get-tuple-element.40), channel_id=1, source_target_pairs={{8,17},{9,16},{10,19},{11,18},{12,21},{13,20},{14,23},{15,22},{16,... | collective-permute-start | bytes 12296 | tf_op jit(solution)/shard_map/ppermute | solution.py:35
  51.5 2.2 %collective-permute-start.15 = (f32[8,128]{1,0:T(8,128)S(1)}, f32[8,128]{1,0:T(8,128)S(1)}, u32[]{:S(2)}, u32[]{:S(2)}) collective-permute-start(f32[8,128]{1,0:T(8,128)S(1)} %get-tuple-element.41), channel_id=1, source_target_pairs={{8,23},{9,18},{10,17},{11,20},{12,19},{13,22},{14,21},{15,16},{16,... | collective-permute-start | bytes 12296 | tf_op jit(solution)/shard_map/ppermute | solution.py:35
